TPU v7x, 512 devices: a whole 4x4x16 slice. The times are simulated.
512 devices in a mesh: dp: 16 (over x, y), seq: 32 (over z, core).
Axes of the slice: x: 4, y: 4, z: 16, core: 2. Of those that a mesh axis runs over, the one named last changes fastest.
Arguments:
- queries: bfloat16 [16, 4096, 4096], P('dp', 'seq'), may hold values from -6 to 6
- key_states: bfloat16 [16, 4096, 1024], P('dp', 'seq'), may hold values from -8 to 8
- value_states: bfloat16 [16, 4096, 1024], P('dp', 'seq'), may hold values from -6 to 6
- sink_logit: float32 [32], P('seq'), may hold values from 7 to 12
- out_grad: bfloat16 [16, 4096, 4096], P('dp', 'seq'), may hold values from -16 to 16
- block_table: int32 [32, 32, 8], P('seq'), may hold values from 0 to 31, as said below
Outputs:
- query_grad: bfloat16 [16, 4096, 4096], P('dp', 'seq')
- key_grad: bfloat16 [16, 4096, 1024], P('dp', 'seq')
- value_grad: bfloat16 [16, 4096, 1024], P('dp', 'seq')
- sink_grad: float32 [32], P('seq')
Inputs may be any that keep to these rules, and one draw needn't show every extreme that they name: `block_table`: each row lists 8 different key blocks; among them are the query's own block, the two blocks beside it (cyclically) and block 0.
All inputs are finite; a program needn't handle non-finite values.
Results may differ from a plain program's by a relative error of at most 0.0066.
Values may be sent and summed in bfloat16 or wider, within the bound.
No kernel may reach another device: no remote copies, remote signals or barrier semaphores. Data moves between devices by JAX's collectives and lax.ppermute only.
A program may use at most 64 MiB of HBM per device.

v0:
```python
import functools

import jax
import jax.numpy as jnp
from jax import lax
from jax.experimental import pallas as pl
from jax.experimental.pallas import tpu as pltpu
from jax.sharding import PartitionSpec as P

HEADS = 32
KV_HEADS = 8
HEAD_DIM = 128
BLOCK = 128
KB = 8
GROUP = HEADS // KV_HEADS
LOG2E = 1.4426950408889634


def kernel(
    core_ref, table_ref, sink_ref, q0_ref, q1_ref, g0_ref, g1_ref, kv_ref,
    dq0_ref, dq1_ref, dkv_ref, dsink_ref, acc_ref, w_ref,
):
    scale = HEAD_DIM**-0.5
    kv_head = pl.program_id(0)
    acc_ref[...] = jnp.zeros_like(acc_ref)
    w_ref[...] = jnp.zeros_like(w_ref)
    for j in range(GROUP):
        columns = slice(j * HEAD_DIM, (j + 1) * HEAD_DIM)
        sink = sink_ref[pl.ds(kv_head * GROUP + j, 1), :] * LOG2E
        sink_terms = jnp.zeros((1, BLOCK), jnp.float32)
        for s, (q_ref, g_ref, dq_ref) in enumerate(
            ((q0_ref, g0_ref, dq0_ref), (q1_ref, g1_ref, dq1_ref))
        ):
            w_ref[s, :BLOCK, :HEAD_DIM] = q_ref[:, columns]
            w_ref[s, BLOCK:, HEAD_DIM:] = g_ref[:, columns]
            w = w_ref[s]
            rows = []
            for b in range(KB):
                block = table_ref[((kv_head * GROUP + j) * 2 + s) * KB + b]
                rows.append(pl.ds(pl.multiple_of(block * BLOCK, BLOCK), BLOCK))
            both = [
                lax.dot_general(
                    kv_ref[r, :], w, (((1,), (1,)), ((), ())),
                    preferred_element_type=jnp.float32,
                )
                for r in rows
            ]
            scores = [x[:, :BLOCK] * (scale * LOG2E) for x in both]
            dprobs = [x[:, BLOCK:] for x in both]
            top = functools.reduce(jnp.maximum, scores)
            top = jnp.maximum(jnp.max(top, 0, keepdims=True), sink)
            weights = [jnp.exp2(x - top) for x in scores]
            sink_weight = jnp.exp2(sink - top)
            total = jnp.sum(functools.reduce(jnp.add, weights), 0, keepdims=True) + sink_weight
            inverse = 1.0 / total
            probs = [x * inverse for x in weights]
            low = [x.astype(jnp.bfloat16) for x in probs]
            delta = functools.reduce(
                jnp.add, [x.astype(jnp.float32) * y for x, y in zip(low, dprobs)]
            )
            delta = jnp.sum(delta, 0, keepdims=True)
            dscores = [(x * (y - delta)).astype(jnp.bfloat16) for x, y in zip(probs, dprobs)]
            dq = jnp.zeros((BLOCK, HEAD_DIM), jnp.float32)
            for b, r in enumerate(rows):
                terms = jnp.concatenate([dscores[b], low[b]], 1)
                acc_ref[r, :] += jnp.dot(terms, w, preferred_element_type=jnp.float32)
                dq += lax.dot_general(
                    dscores[b], kv_ref[r, :HEAD_DIM], (((0,), (0,)), ((), ())),
                    preferred_element_type=jnp.float32,
                )
            dq_ref[:, columns] = (dq * scale).astype(jnp.bfloat16)
            sink_terms -= sink_weight * inverse * delta
        dsink_ref[pl.ds(kv_head * GROUP + j, 1), :] = sink_terms
    dkv_ref[:, :HEAD_DIM] = (acc_ref[:, :HEAD_DIM] * scale).astype(jnp.bfloat16)
    dkv_ref[:, HEAD_DIM:] = acc_ref[:, HEAD_DIM:].astype(jnp.bfloat16)


def attention(core, table, sink, queries, q_other, grads, g_other, kv):
    length = kv.shape[0]
    kv_heads = KV_HEADS // 2
    wide = GROUP * HEAD_DIM
    own = lambda g, core, table: (0, core[0] * kv_heads + g)
    at = lambda g, core, table: (0, g)
    fixed = lambda g, core, table: (0, 0)
    heads = HEADS // 2
    return pl.pallas_call(
        kernel,
        grid_spec=pltpu.PrefetchScalarGridSpec(
            num_scalar_prefetch=2,
            grid=(kv_heads,),
            in_specs=[
                pl.BlockSpec((heads, BLOCK), fixed),
                pl.BlockSpec((BLOCK, wide), own),
                pl.BlockSpec((BLOCK, wide), at),
                pl.BlockSpec((BLOCK, wide), own),
                pl.BlockSpec((BLOCK, wide), at),
                pl.BlockSpec((length, 2 * HEAD_DIM), at),
            ],
            out_specs=[
                pl.BlockSpec((BLOCK, wide), at),
                pl.BlockSpec((BLOCK, wide), at),
                pl.BlockSpec((length, 2 * HEAD_DIM), at),
                pl.BlockSpec((heads, BLOCK), fixed),
            ],
            scratch_shapes=[
                pltpu.VMEM((length, 2 * HEAD_DIM), jnp.float32),
                pltpu.VMEM((2, 2 * BLOCK, 2 * HEAD_DIM), jnp.bfloat16),
            ],
        ),
        out_shape=[
            jax.ShapeDtypeStruct((BLOCK, kv_heads * wide), jnp.bfloat16),
            jax.ShapeDtypeStruct((BLOCK, kv_heads * wide), jnp.bfloat16),
            jax.ShapeDtypeStruct((length, kv_heads * 2 * HEAD_DIM), jnp.bfloat16),
            jax.ShapeDtypeStruct((heads, BLOCK), jnp.float32),
        ],
        compiler_params=pltpu.CompilerParams(vmem_limit_bytes=48 * 2**20),
        cost_estimate=pl.CostEstimate(
            flops=2 * 5 * heads * 2 * BLOCK * KB * BLOCK * HEAD_DIM,
            bytes_accessed=2 * 2 * length * kv_heads * 2 * HEAD_DIM,
            transcendentals=heads * 2 * BLOCK * KB * BLOCK,
        ),
    )(core, table, sink, queries, q_other, grads, g_other, kv)


def shards(queries, key_states, value_states, sink_logit, out_grad, block_table):
    devices = lax.axis_size("seq")
    chips = devices // 2
    me = lax.axis_index("seq")
    core = me % 2
    half_kv = KV_HEADS // 2
    half = HEADS // 2
    swap = lambda x: lax.ppermute(x, "seq", [(i, i ^ 1) for i in range(devices)])
    groups = [list(range(0, devices, 2)), list(range(1, devices, 2))]

    def halves(x, which, width):
        return lax.dynamic_slice_in_dim(x, which * width, width, axis=1)

    kv = jnp.stack(
        [
            key_states.reshape(BLOCK, KV_HEADS, HEAD_DIM),
            value_states.reshape(BLOCK, KV_HEADS, HEAD_DIM),
        ],
        2,
    ).reshape(BLOCK, KV_HEADS * 2 * HEAD_DIM)
    kv_width = half_kv * 2 * HEAD_DIM
    kv_own = halves(kv, core, kv_width)
    kv_other = swap(halves(kv, 1 - core, kv_width))
    kv_chip = jnp.concatenate([kv_own, kv_other], 0)
    kv_all = lax.all_gather(kv_chip, "seq", axis=0, tiled=True, axis_index_groups=groups)

    q_local = queries.reshape(BLOCK, HEADS * HEAD_DIM)
    g_local = out_grad.reshape(BLOCK, HEADS * HEAD_DIM)
    q_other = swap(halves(q_local, 1 - core, half * HEAD_DIM))
    g_other = swap(halves(g_local, 1 - core, half * HEAD_DIM))

    blocks = block_table.shape[1]
    info = jnp.concatenate(
        [
            block_table.astype(jnp.float32).reshape(blocks, KB),
            jnp.broadcast_to(sink_logit.reshape(1, 1), (blocks, 1)),
        ],
        1,
    ).reshape(chips, 1, 2 * (KB + 1))
    info = jnp.broadcast_to(info, (chips, 2, 2 * (KB + 1))).reshape(devices, 2 * (KB + 1))
    info = lax.all_to_all(info, "seq", split_axis=0, concat_axis=0, tiled=True)
    info = lax.dynamic_slice_in_dim(info, core * half, half, axis=0).reshape(half, 2, KB + 1)
    table = info[:, :, :KB].astype(jnp.int32)
    table = jnp.where(core == 0, table, table[:, ::-1]) ^ core
    sink = jnp.broadcast_to(info[:, 0, KB:], (half, BLOCK))

    dq_own, dq_other, dkv, dsink = attention(
        core.reshape(1).astype(jnp.int32), table.reshape(-1), sink,
        q_local, q_other, g_local, g_other, kv_all,
    )

    dkv_chip = lax.psum_scatter(
        dkv, "seq", scatter_dimension=0, tiled=True, axis_index_groups=groups
    )
    dkv_back = swap(dkv_chip[BLOCK:])
    first = jnp.where(core == 0, dkv_chip[:BLOCK], dkv_back)
    second = jnp.where(core == 0, dkv_back, dkv_chip[:BLOCK])
    dkv_full = jnp.concatenate([first, second], 1).reshape(BLOCK, KV_HEADS, 2, HEAD_DIM)
    key_grad = dkv_full[:, :, 0].reshape(1, BLOCK, KV_HEADS * HEAD_DIM)
    value_grad = dkv_full[:, :, 1].reshape(1, BLOCK, KV_HEADS * HEAD_DIM)

    dq_back = swap(dq_other)
    query_grad = jnp.concatenate(
        [jnp.where(core == 0, dq_own, dq_back), jnp.where(core == 0, dq_back, dq_own)], 1
    ).reshape(1, BLOCK, HEADS * HEAD_DIM)

    total = jnp.sum(dsink, 1).reshape(1, half)
    for step in (1, 2, 4, 8):
        total += lax.ppermute(total, "dp", [(i, i ^ step) for i in range(16)])
    for step in (2, 4, 8, 16):
        total += lax.ppermute(total, "seq", [(i, i ^ step) for i in range(devices)])
    other = swap(total)
    sinks = jnp.concatenate(
        [jnp.where(core == 0, total, other), jnp.where(core == 0, other, total)], 1
    )
    sink_grad = lax.dynamic_slice_in_dim(sinks.reshape(HEADS), me, 1)
    return (query_grad, key_grad, value_grad, sink_grad)


def solution(mesh):
    in_specs = (
        P("dp", "seq", None),
        P("dp", "seq", None),
        P("dp", "seq", None),
        P("seq"),
        P("dp", "seq", None),
        P("seq", None, None),
    )
    out_specs = (P("dp", "seq", None), P("dp", "seq", None), P("dp", "seq", None), P("seq"))
    return jax.shard_map(shards, mesh=mesh, in_specs=in_specs, out_specs=out_specs, check_vma=False)
```

profile of v0, /device:TPU:1, one launch (start us, length us, event | category | flops | bytes accessed | tf_op | source)
XLA Modules:
  0.0 287.6 jit_solution(7706244151784845614)
XLA Ops:
  11.2 8.9 %collective-permute-start.2 = (bf16[128,1024]{1,0:T(8,128)(2,1)S(1)}, bf16[128,1024]{1,0:T(8,128)(2,1)S(1)}, u32[]{:S(2)}, u32[]{:S(2)}) collective-permute-start(bf16[128,1024]{1,0:T(8,128)(2,1)S(1)} %get-tuple-element.31), channel_id=1, source_target_pairs={{0,1},{1,0},{2,3},{3,2},{4,5},{5,4},{6,7},{7,6},{8,9},{9,8},{10,11... | collective-permute-start | bytes 786440 | tf_op jit(solution)/shard_map/ppermute | solution.py:132
  23.6 10.2 %all-to-all-start = ((f32[32,1,18]{2,1,0:T(1,128)}), f32[32,1,18]{2,1,0:T(1,128)S(1)}, u32[]{:S(2)}, u32[]{:S(2)}) async-start(f32[32,1,18]{2,1,0:T(1,128)} %bitcast.4), calls=%async_computation | async-start | bytes 32768 | tf_op jit(solution)/shard_map/all_to_all | solution.py:165
  34.8 2.1 collective-permute-start.1
  37.8 2.2 collective-permute-start
  40.0 5.7 %all-to-all-done = f32[32,1,18]{2,1,0:T(1,128)S(1)} async-done(((f32[32,1,18]{2,1,0:T(1,128)}), f32[32,1,18]{2,1,0:T(1,128)S(1)}, u32[]{:S(2)}, u32[]{:S(2)}) %all-to-all-start) | async-done | bytes 2336 | tf_op jit(solution)/shard_map/all_to_all | solution.py:165
  47.8 79.5 %all-gather.2.cloned.1.call-done.kv_ref = bf16[4096,1024]{1,0:T(8,128)(2,1)} async-done(((bf16[256,1024]{1,0:T(8,128)(2,1)}), bf16[4096,1024]{1,0:T(8,128)(2,1)}) %all-gather.2.cloned.1.call-update) | async-done | bytes 8388624 | tf_op jit(solution)/shard_map/all_gather | solution.py:149
  129.4 38.7 %shard_map.93 = (bf16[128,2048]{1,0:T(8,128)(2,1)S(1)}, bf16[128,2048]{1,0:T(8,128)(2,1)S(1)}, bf16[4096,1024]{1,0:T(8,128)(2,1)}, f32[16,128]{1,0:T(8,128)S(1)}) custom-call(s32[1]{0:T(128)} %bitcast.core_ref, s32[256]{0:T(256)S(1)} %reshape.58.table_ref, f32[16,128]{1,0:T(8,128)S(1)} %broadcast_in_dim.23.sink_ref, bf16[128,4096]{1,0:T(8,128)(2,1)S(1)} %bitcast.21, ...), custom_call_target="tpu_custom_call" | custom-call | flops 5368709120 | bytes 16777216 | tf_op jit(solution)/shard_map/pallas_call | solution.py:86
  168.3 3.1 %collective-permute-start.5 = (f32[1,16]{1,0:T(1,128)S(1)}, f32[1,16]{1,0:T(1,128)S(1)}, u32[]{:S(2)}, u32[]{:S(2)}) collective-permute-start(f32[1,16]{1,0:T(1,128)S(1)} %bitcast.25), channel_id=1, source_target_pairs={{0,32},{32,0},{64,96},{96,64},{128,160},{160,128},{192,224},{224,1... | collective-permute-start | bytes 200 | tf_op jit(solution)/shard_map/ppermute | solution.py:193
  171.4 2.9 collective-permute-start.3
  174.3 4.3 %collective-permute-start.6 = (f32[1,16]{1,0:T(1,128)S(1)}, f32[1,16]{1,0:T(1,128)S(1)}, u32[]{:S(2)}, u32[]{:S(2)}) collective-permute-start(f32[1,16]{1,0:T(1,128)S(1)} %bitcast_add_fusion), channel_id=1, source_target_pairs={{0,64},{32,96},{64,0},{96,32},{128,192},{160,224},{192,128},{224,1... | collective-permute-start | bytes 200 | tf_op jit(solution)/shard_map/ppermute | solution.py:193
  178.6 1.5 collective-permute-done.6
  180.1 3.1 %collective-permute-start.7 = (f32[1,16]{1,0:T(1,128)S(1)}, f32[1,16]{1,0:T(1,128)S(1)}, u32[]{:S(2)}, u32[]{:S(2)}) collective-permute-start(f32[1,16]{1,0:T(1,128)S(1)} %add.54), channel_id=1, source_target_pairs={{0,128},{32,160},{64,192},{96,224},{128,0},{160,32},{192,64},{224,... | collective-permute-start | bytes 200 | tf_op jit(solution)/shard_map/ppermute | solution.py:193
  184.4 4.6 %collective-permute-start.8 = (f32[1,16]{1,0:T(1,128)S(1)}, f32[1,16]{1,0:T(1,128)S(1)}, u32[]{:S(2)}, u32[]{:S(2)}) collective-permute-start(f32[1,16]{1,0:T(1,128)S(1)} %add.55), channel_id=1, source_target_pairs={{0,256},{32,288},{64,320},{96,352},{128,384},{160,416},{192,448},{... | collective-permute-start | bytes 200 | tf_op jit(solution)/shard_map/ppermute | solution.py:193
  190.2 1.9 collective-permute-start.9
  192.1 2.9 %collective-permute-done.9 = f32[1,16]{1,0:T(1,128)S(1)} collective-permute-done((f32[1,16]{1,0:T(1,128)S(1)}, f32[1,16]{1,0:T(1,128)S(1)}, u32[]{:S(2)}, u32[]{:S(2)}) %collective-permute-start.9) | collective-permute-done | bytes 96 | tf_op jit(solution)/shard_map/ppermute | solution.py:195
  195.1 2.5 collective-permute-start.10
  197.6 3.2 %collective-permute-done.10 = f32[1,16]{1,0:T(1,128)S(1)} collective-permute-done((f32[1,16]{1,0:T(1,128)S(1)}, f32[1,16]{1,0:T(1,128)S(1)}, u32[]{:S(2)}, u32[]{:S(2)}) %collective-permute-start.10) | collective-permute-done | bytes 96 | tf_op jit(solution)/shard_map/ppermute | solution.py:195
  200.8 5.4 %collective-permute-start.11 = (f32[1,16]{1,0:T(1,128)S(1)}, f32[1,16]{1,0:T(1,128)S(1)}, u32[]{:S(2)}, u32[]{:S(2)}) collective-permute-start(f32[1,16]{1,0:T(1,128)S(1)} %add.58), channel_id=1, source_target_pairs={{0,8},{1,9},{2,10},{3,11},{4,12},{5,13},{6,14},{7,15},{8,0},{9,1},... | collective-permute-start | bytes 200 | tf_op jit(solution)/shard_map/ppermute | solution.py:195
  206.3 2.9 %collective-permute-done.11 = f32[1,16]{1,0:T(1,128)S(1)} collective-permute-done((f32[1,16]{1,0:T(1,128)S(1)}, f32[1,16]{1,0:T(1,128)S(1)}, u32[]{:S(2)}, u32[]{:S(2)}) %collective-permute-start.11) | collective-permute-done | bytes 96 | tf_op jit(solution)/shard_map/ppermute | solution.py:195
  209.2 8.9 %collective-permute-start.12 = (f32[1,16]{1,0:T(1,128)S(1)}, f32[1,16]{1,0:T(1,128)S(1)}, u32[]{:S(2)}, u32[]{:S(2)}) collective-permute-start(f32[1,16]{1,0:T(1,128)S(1)} %add.59), channel_id=1, source_target_pairs={{0,16},{1,17},{2,18},{3,19},{4,20},{5,21},{6,22},{7,23},{8,24},{9,... | collective-permute-start | bytes 200 | tf_op jit(solution)/shard_map/ppermute | solution.py:195
  218.1 4.3 %collective-permute-done.12 = f32[1,16]{1,0:T(1,128)S(1)} collective-permute-done((f32[1,16]{1,0:T(1,128)S(1)}, f32[1,16]{1,0:T(1,128)S(1)}, u32[]{:S(2)}, u32[]{:S(2)}) %collective-permute-start.12) | collective-permute-done | bytes 96 | tf_op jit(solution)/shard_map/ppermute | solution.py:195
  222.4 9.1 %collective-permute-start.13 = (f32[1,16]{1,0:T(1,128)S(1)}, f32[1,16]{1,0:T(1,128)S(1)}, u32[]{:S(2)}, u32[]{:S(2)}) collective-permute-start(f32[1,16]{1,0:T(1,128)S(1)} %add.60), channel_id=1, source_target_pairs={{0,1},{1,0},{2,3},{3,2},{4,5},{5,4},{6,7},{7,6},{8,9},{9,8},{10,11... | collective-permute-start | bytes 200 | tf_op jit(solution)/shard_map/ppermute | solution.py:132
  233.1 39.2 %reduce-scatter.2.cloned.1.call-done = bf16[256,1024]{1,0:T(8,128)(2,1)} async-done(((bf16[4096,1024]{1,0:T(8,128)(2,1)}), bf16[256,1024]{1,0:T(8,128)(2,1)}) %reduce-scatter.2.cloned.1.call-update) | async-done | bytes 524304 | tf_op jit(solution)/shard_map/reduce_scatter | solution.py:176
  273.3 2.5 collective-permute-start.4
  (73 shorter events, 22.9 us)
Async XLA Ops:
  7.2 120.1 %all-gather.2.cloned.1.call-start = ((), (), s32[]{:S(2)}) async-start(), calls=%async_computation.2 | async-start | bytes 8912896 | tf_op jit(solution)/shard_map/all_gather | solution.py:149
  10.7 12.1 %copy-start.7 = (s32[1,32,8]{1,2,0:T(8,128)S(1)}, s32[1,32,8]{1,2,0:T(8,128)}, u32[]{:S(2)}) copy-start(s32[1,32,8]{1,2,0:T(8,128)} %param.11) | copy-start | bytes 3076
  10.7 23.2 %copy-start.1 = (bf16[1,128,4096]{2,1,0:T(8,128)(2,1)S(1)}, bf16[1,128,4096]{2,1,0:T(8,128)(2,1)}, u32[]{:S(2)}) copy-start(bf16[1,128,4096]{2,1,0:T(8,128)(2,1)} %param.10) | copy-start | bytes 3145732
  11.1 25.8 %copy-start = (bf16[1,128,4096]{2,1,0:T(8,128)(2,1)S(1)}, bf16[1,128,4096]{2,1,0:T(8,128)(2,1)}, u32[]{:S(2)}) copy-start(bf16[1,128,4096]{2,1,0:T(8,128)(2,1)} %param.6) | copy-start | bytes 3145732
  11.2 10.1 %collective-permute-start.2 = (bf16[128,1024]{1,0:T(8,128)(2,1)S(1)}, bf16[128,1024]{1,0:T(8,128)(2,1)S(1)}, u32[]{:S(2)}, u32[]{:S(2)}) collective-permute-start(bf16[128,1024]{1,0:T(8,128)(2,1)S(1)} %get-tuple-element.31), channel_id=1, source_target_pairs={{0,1},{1,0},{2,3},{3,2},{4,5},{5,4},{6,7},{7,6},{8,9},{9,8},{10,11... | collective-permute-start | bytes 786440 | tf_op jit(solution)/shard_map/ppermute | solution.py:132
  23.6 22.0 %all-to-all-start = ((f32[32,1,18]{2,1,0:T(1,128)}), f32[32,1,18]{2,1,0:T(1,128)S(1)}, u32[]{:S(2)}, u32[]{:S(2)}) async-start(f32[32,1,18]{2,1,0:T(1,128)} %bitcast.4), calls=%async_computation | async-start | bytes 32768 | tf_op jit(solution)/shard_map/all_to_all | solution.py:165
  33.9 238.4 %reduce-scatter.2.cloned.1.call-start = ((), (), s32[]{:S(2)}) async-start(), calls=%async_computation.3 | async-start | bytes 8912896 | tf_op jit(solution)/shard_map/reduce_scatter | solution.py:176
  34.8 11.4 %collective-permute-start.1 = (bf16[128,2048]{1,0:T(8,128)(2,1)}, bf16[128,2048]{1,0:T(8,128)(2,1)S(1)}, u32[]{:S(2)}, u32[]{:S(2)}) collective-permute-start(bf16[128,2048]{1,0:T(8,128)(2,1)} %dynamic-slice_bitcast_fusion), channel_id=1, source_target_pairs={{0,1},{1,0},{2,3},{3,2},{4,5},{5,4},{6,7},{7,6},{8,9},{9,8},{10,11... | collective-permute-start | bytes 1572872 | tf_op jit(solution)/shard_map/ppermute | solution.py:132
  37.8 9.2 %collective-permute-start = (bf16[128,2048]{1,0:T(8,128)(2,1)}, bf16[128,2048]{1,0:T(8,128)(2,1)S(1)}, u32[]{:S(2)}, u32[]{:S(2)}) collective-permute-start(bf16[128,2048]{1,0:T(8,128)(2,1)} %dynamic-slice_bitcast_fusion.1), channel_id=1, source_target_pairs={{0,1},{1,0},{2,3},{3,2},{4,5},{5,4},{6,7},{7,6},{8,9},{9,8},{10,11... | collective-permute-start | bytes 1572872 | tf_op jit(solution)/shard_map/ppermute | solution.py:132
  46.2 0.8 copy-start.2
  127.3 1.0 copy-start.3
  128.4 1.0 copy-start.5
  168.3 6.0 %collective-permute-start.5 = (f32[1,16]{1,0:T(1,128)S(1)}, f32[1,16]{1,0:T(1,128)S(1)}, u32[]{:S(2)}, u32[]{:S(2)}) collective-permute-start(f32[1,16]{1,0:T(1,128)S(1)} %bitcast.25), channel_id=1, source_target_pairs={{0,32},{32,0},{64,96},{96,64},{128,160},{160,128},{192,224},{224,1... | collective-permute-start | bytes 200 | tf_op jit(solution)/shard_map/ppermute | solution.py:193
  171.4 61.6 %collective-permute-start.3 = (bf16[128,2048]{1,0:T(8,128)(2,1)S(1)}, bf16[128,2048]{1,0:T(8,128)(2,1)S(1)}, u32[]{:S(2)}, u32[]{:S(2)}) collective-permute-start(bf16[128,2048]{1,0:T(8,128)(2,1)S(1)} %get-tuple-element.9), channel_id=1, source_target_pairs={{0,1},{1,0},{2,3},{3,2},{4,5},{5,4},{6,7},{7,6},{8,9},{9,8},{10,11... | collective-permute-start | bytes 1572872 | tf_op jit(solution)/shard_map/ppermute | solution.py:132
  174.3 5.8 %collective-permute-start.6 = (f32[1,16]{1,0:T(1,128)S(1)}, f32[1,16]{1,0:T(1,128)S(1)}, u32[]{:S(2)}, u32[]{:S(2)}) collective-permute-start(f32[1,16]{1,0:T(1,128)S(1)} %bitcast_add_fusion), channel_id=1, source_target_pairs={{0,64},{32,96},{64,0},{96,32},{128,192},{160,224},{192,128},{224,1... | collective-permute-start | bytes 200 | tf_op jit(solution)/shard_map/ppermute | solution.py:193
  180.1 4.3 %collective-permute-start.7 = (f32[1,16]{1,0:T(1,128)S(1)}, f32[1,16]{1,0:T(1,128)S(1)}, u32[]{:S(2)}, u32[]{:S(2)}) collective-permute-start(f32[1,16]{1,0:T(1,128)S(1)} %add.54), channel_id=1, source_target_pairs={{0,128},{32,160},{64,192},{96,224},{128,0},{160,32},{192,64},{224,... | collective-permute-start | bytes 200 | tf_op jit(solution)/shard_map/ppermute | solution.py:193
  184.4 5.9 %collective-permute-start.8 = (f32[1,16]{1,0:T(1,128)S(1)}, f32[1,16]{1,0:T(1,128)S(1)}, u32[]{:S(2)}, u32[]{:S(2)}) collective-permute-start(f32[1,16]{1,0:T(1,128)S(1)} %add.55), channel_id=1, source_target_pairs={{0,256},{32,288},{64,320},{96,352},{128,384},{160,416},{192,448},{... | collective-permute-start | bytes 200 | tf_op jit(solution)/shard_map/ppermute | solution.py:193
  190.2 4.8 %collective-permute-start.9 = (f32[1,16]{1,0:T(1,128)S(1)}, f32[1,16]{1,0:T(1,128)S(1)}, u32[]{:S(2)}, u32[]{:S(2)}) collective-permute-start(f32[1,16]{1,0:T(1,128)S(1)} %add.56), channel_id=1, source_target_pairs={{0,2},{1,3},{2,0},{3,1},{4,6},{5,7},{6,4},{7,5},{8,10},{9,11},{10,... | collective-permute-start | bytes 200 | tf_op jit(solution)/shard_map/ppermute | solution.py:195
  195.1 5.7 %collective-permute-start.10 = (f32[1,16]{1,0:T(1,128)S(1)}, f32[1,16]{1,0:T(1,128)S(1)}, u32[]{:S(2)}, u32[]{:S(2)}) collective-permute-start(f32[1,16]{1,0:T(1,128)S(1)} %add.57), channel_id=1, source_target_pairs={{0,4},{1,5},{2,6},{3,7},{4,0},{5,1},{6,2},{7,3},{8,12},{9,13},{10,... | collective-permute-start | bytes 200 | tf_op jit(solution)/shard_map/ppermute | solution.py:195
  200.8 8.4 %collective-permute-start.11 = (f32[1,16]{1,0:T(1,128)S(1)}, f32[1,16]{1,0:T(1,128)S(1)}, u32[]{:S(2)}, u32[]{:S(2)}) collective-permute-start(f32[1,16]{1,0:T(1,128)S(1)} %add.58), channel_id=1, source_target_pairs={{0,8},{1,9},{2,10},{3,11},{4,12},{5,13},{6,14},{7,15},{8,0},{9,1},... | collective-permute-start | bytes 200 | tf_op jit(solution)/shard_map/ppermute | solution.py:195
  209.2 13.2 %collective-permute-start.12 = (f32[1,16]{1,0:T(1,128)S(1)}, f32[1,16]{1,0:T(1,128)S(1)}, u32[]{:S(2)}, u32[]{:S(2)}) collective-permute-start(f32[1,16]{1,0:T(1,128)S(1)} %add.59), channel_id=1, source_target_pairs={{0,16},{1,17},{2,18},{3,19},{4,20},{5,21},{6,22},{7,23},{8,24},{9,... | collective-permute-start | bytes 200 | tf_op jit(solution)/shard_map/ppermute | solution.py:195
  222.4 9.9 %collective-permute-start.13 = (f32[1,16]{1,0:T(1,128)S(1)}, f32[1,16]{1,0:T(1,128)S(1)}, u32[]{:S(2)}, u32[]{:S(2)}) collective-permute-start(f32[1,16]{1,0:T(1,128)S(1)} %add.60), channel_id=1, source_target_pairs={{0,1},{1,0},{2,3},{3,2},{4,5},{5,4},{6,7},{7,6},{8,9},{9,8},{10,11... | collective-permute-start | bytes 200 | tf_op jit(solution)/shard_map/ppermute | solution.py:132
  272.2 4.7 %copy-start.6 = (bf16[256,1024]{1,0:T(8,128)(2,1)S(1)}, bf16[256,1024]{1,0:T(8,128)(2,1)}, u32[]{:S(2)}) copy-start(bf16[256,1024]{1,0:T(8,128)(2,1)} %reduce-scatter.2.cloned.1.call-done) | copy-start | bytes 1572868
  273.3 3.7 %collective-permute-start.4 = (bf16[128,1024]{1,0:T(8,128)(2,1)S(1)}, bf16[128,1024]{1,0:T(8,128)(2,1)S(1)}, u32[]{:S(2)}, u32[]{:S(2)}) collective-permute-start(bf16[128,1024]{1,0:T(8,128)(2,1)S(1)} %slice.28), channel_id=1, source_target_pairs={{0,1},{1,0},{2,3},{3,2},{4,5},{5,4},{6,7},{7,6},{8,9},{9,8},{10,11... | collective-permute-start | bytes 786440 | tf_op jit(solution)/shard_map/ppermute | solution.py:132
  (1 other events, 0.8 us)
Sparse Core Ops, SparseCore 0:
  22.3 104.9 all-gather.1
  168.3 103.9 reduce-scatter.1
where the time goes:
time: 288 us
  waiting for transfers between devices  144 us (50%)
  starting transfers between devices  71.9 us (25%)
  Pallas kernels  38.7 us (13%)
  between operations  15.1 us (5%)
  local copies, waits for them, and re-layouts  14.7 us (5%)
  other arithmetic  3.53 us (1%)
    all_gather x1, waiting for transfers between devices, shards(): lax.all_gather(kv_chip, 'seq', axis=0, tiled=True, axis_index_groups=groups)  79.5 us
    reduce_scatter x1, waiting for transfers between devices, shards(): lax.psum_scatter(dkv, 'seq', scatter_dimension=0, tiled=True, axis_index_...  39.2 us
    pallas_call x1, Pallas kernels, attention(): pl.pallas_call(kernel, grid_spec=pltpu.PrefetchScalarGridSpec(num_scalar_...  38.7 us
    ppermute x6, starting transfers between devices, shards(): lax.ppermute(x, 'seq', [(i, i ^ 1) for i in range(devices)])  27.8 us
    ppermute x4, starting transfers between devices, shards(): total += lax.ppermute(total, 'seq', [(i, i ^ step) for i in range(devices)])  18.7 us
    ppermute x4, starting transfers between devices, shards(): total += lax.ppermute(total, 'dp', [(i, i ^ step) for i in range(16)])  15.1 us
    ppermute x4, waiting for transfers between devices, shards(): total += lax.ppermute(total, 'seq', [(i, i ^ step) for i in range(devices)])  13.4 us
    all_to_all x1, starting transfers between devices, shards(): info = lax.all_to_all(info, 'seq', split_axis=0, concat_axis=0, tiled=True)  10.2 us
  transfers between devices with their start and end apart: 17, of which 13 were waited for; matrix products, arithmetic and copies ran while one was open for 2% of the time, Pallas kernels for 0%

commit v1 on v0

v1 whole, which is shorter than its diff:
```python
import functools

import jax
import jax.numpy as jnp
from jax import lax
from jax.experimental import pallas as pl
from jax.experimental.pallas import tpu as pltpu
from jax.sharding import PartitionSpec as P

HEADS = 32
KV_HEADS = 8
HEAD_DIM = 128
BLOCK = 128
KB = 8
GROUP = HEADS // KV_HEADS
LOG2E = 1.4426950408889634
SCALE = HEAD_DIM**-0.5
UNROLL = 4


def kernel(
    base, core_ref, table_ref, sink_ref, q0_ref, q1_ref, g0_ref, g1_ref,
    qt0_ref, qt1_ref, gt0_ref, gt1_ref, kv_ref,
    dq0_ref, dq1_ref, dkv_ref, dsink_ref, acc_ref, w_ref, wt_ref, kt_ref,
):
    chips = kv_ref.shape[0]
    local = pl.program_id(0)
    kv_head = base + local
    acc_ref[...] = jnp.zeros_like(acc_ref)
    w_ref[...] = jnp.zeros_like(w_ref)
    wt_ref[...] = jnp.zeros_like(wt_ref)
    for c in range(chips):
        for s in range(2):
            kt_ref[c, s] = kv_ref[c, 0, s * BLOCK : (s + 1) * BLOCK, :].T
    refs = (
        (q0_ref, g0_ref, qt0_ref, gt0_ref, dq0_ref),
        (q1_ref, g1_ref, qt1_ref, gt1_ref, dq1_ref),
    )

    def several(step, _):
        def first(u, s):
            j = step * UNROLL + u
            i = (2 * u + s) % 4
            at = pl.ds(pl.multiple_of(j * HEAD_DIM, HEAD_DIM), HEAD_DIM)
            q_ref, g_ref, qt_ref, gt_ref, _ = refs[s]
            w_ref[i, :BLOCK, :HEAD_DIM] = q_ref[:, at]
            w_ref[i, BLOCK:, HEAD_DIM:] = g_ref[:, at]
            wt_ref[i, :HEAD_DIM, :BLOCK] = qt_ref[at, :]
            wt_ref[i, HEAD_DIM:, BLOCK:] = gt_ref[at, :]
            wt = wt_ref[i]
            places, both = [], []
            for b in range(KB):
                block = table_ref[((kv_head * GROUP + j) * 2 + s) * KB + b]
                chip, slot = block >> 1, block & 1
                rows = pl.ds(pl.multiple_of(slot * BLOCK, BLOCK), BLOCK)
                places.append((chip, slot, rows))
                kv = jnp.concatenate([kv_ref[chip, 0, rows, :], kv_ref[chip, 1, rows, :]], 1)
                both.append(jnp.dot(kv, wt, preferred_element_type=jnp.float32))
            sink = sink_ref[pl.ds(kv_head * GROUP + j, 1), :] * LOG2E
            return at, places, both, sink

        def middle(both, sink):
            scores = [x[:, :BLOCK] for x in both]
            dprobs = [x[:, BLOCK:] for x in both]
            top = jnp.max(functools.reduce(jnp.maximum, scores), 0, keepdims=True)
            top = jnp.maximum(top * (SCALE * LOG2E), sink)
            sink_weight = jnp.exp2(sink - top)
            total = jnp.zeros((BLOCK, BLOCK), jnp.float32)
            delta = jnp.zeros((BLOCK, BLOCK), jnp.float32)
            weights = []
            for x, y in zip(scores, dprobs):
                weight = jnp.exp2(x * (SCALE * LOG2E) - top)
                total += weight
                delta += weight * y
                weights.append(weight)
            inverse = 1.0 / (jnp.sum(total, 0, keepdims=True) + sink_weight)
            delta = jnp.sum(delta, 0, keepdims=True) * inverse
            terms = []
            for x, y in zip(weights, dprobs):
                probs = x * inverse
                dscores = (probs * (y - delta)).astype(jnp.bfloat16)
                terms.append((dscores, probs.astype(jnp.bfloat16)))
            return terms, sink_weight * inverse * delta

        def last(i, s, at, places, terms):
            w = w_ref[i]
            for (chip, _, rows), pair in zip(places, terms):
                acc_ref[chip, rows, :] += jnp.dot(
                    jnp.concatenate(pair, 1), w, preferred_element_type=jnp.float32
                )
            dq = jnp.zeros((HEAD_DIM, BLOCK), jnp.float32)
            for b in range(0, KB, 2):
                (chip0, slot0, _), (chip1, slot1, _) = places[b], places[b + 1]
                kt = jnp.concatenate([kt_ref[chip0, slot0], kt_ref[chip1, slot1]], 1)
                ds = jnp.concatenate([terms[b][0], terms[b + 1][0]], 0)
                dq += jnp.dot(kt, ds, preferred_element_type=jnp.float32)
            refs[s][4][at, :] = (dq * SCALE).astype(jnp.bfloat16)

        count = 2 * UNROLL
        held = first(0, 0)
        sinks = []
        for k in range(count):
            later = first((k + 1) // 2, (k + 1) % 2) if k + 1 < count else None
            at, places, both, sink = held
            terms, sink_term = middle(both, sink)
            sinks.append(sink_term)
            last(k % 4, k % 2, at, places, terms)
            held = later
        for u in range(UNROLL):
            row = pl.ds(local * GROUP + step * UNROLL + u, 1)
            dsink_ref[row, :] = -(sinks[2 * u] + sinks[2 * u + 1])
        return 0

    lax.fori_loop(0, GROUP // UNROLL, several, 0)
    dkv_ref[:, 0] = (acc_ref[:, :, :HEAD_DIM] * SCALE).astype(dkv_ref.dtype)
    dkv_ref[:, 1] = acc_ref[:, :, HEAD_DIM:].astype(dkv_ref.dtype)


def attention(base, kind, core, table, sink, q, q_other, g, g_other, kv):
    chips, heads_here = kv.shape[0], kv.shape[3] // HEAD_DIM
    kv_heads = KV_HEADS // 2
    wide = GROUP * HEAD_DIM
    half = HEADS // 2
    fixed = lambda i, core, table: (0, 0)
    big = pl.BlockSpec((chips, 2, 2 * BLOCK, HEAD_DIM), lambda i, core, table: (0, 0, 0, i))
    own = pl.BlockSpec((BLOCK, wide), lambda i, core, table: (0, core[0] * kv_heads + base + i))
    other = pl.BlockSpec((BLOCK, wide), lambda i, core, table: (0, base + i))
    own_t = pl.BlockSpec((wide, BLOCK), lambda i, core, table: (core[0] * kv_heads + base + i, 0))
    other_t = pl.BlockSpec((wide, BLOCK), lambda i, core, table: (base + i, 0))
    out_t = pl.BlockSpec((wide, BLOCK), lambda i, core, table: (i, 0))
    pairs = heads_here * GROUP * 2
    return pl.pallas_call(
        functools.partial(kernel, base),
        grid_spec=pltpu.PrefetchScalarGridSpec(
            num_scalar_prefetch=2,
            grid=(heads_here,),
            in_specs=[
                pl.BlockSpec((half, BLOCK), fixed),
                own, other, own, other, own_t, other_t, own_t, other_t, big,
            ],
            out_specs=[out_t, out_t, big, pl.BlockSpec((heads_here * GROUP, BLOCK), fixed)],
            scratch_shapes=[
                pltpu.VMEM((chips, 2 * BLOCK, 2 * HEAD_DIM), jnp.float32),
                pltpu.VMEM((4, 2 * BLOCK, 2 * HEAD_DIM), jnp.bfloat16),
                pltpu.VMEM((4, 2 * HEAD_DIM, 2 * BLOCK), jnp.bfloat16),
                pltpu.VMEM((chips, 2, HEAD_DIM, BLOCK), jnp.bfloat16),
            ],
        ),
        out_shape=[
            jax.ShapeDtypeStruct((heads_here * wide, BLOCK), jnp.bfloat16),
            jax.ShapeDtypeStruct((heads_here * wide, BLOCK), jnp.bfloat16),
            jax.ShapeDtypeStruct((chips, 2, 2 * BLOCK, heads_here * HEAD_DIM), kind),
            jax.ShapeDtypeStruct((heads_here * GROUP, BLOCK), jnp.float32),
        ],
        compiler_params=pltpu.CompilerParams(vmem_limit_bytes=58 * 2**20),
        cost_estimate=pl.CostEstimate(
            flops=2 * 10 * pairs * BLOCK * KB * BLOCK * HEAD_DIM,
            bytes_accessed=2 * 2 * chips * 2 * 2 * BLOCK * heads_here * HEAD_DIM,
            transcendentals=pairs * BLOCK * KB * BLOCK,
        ),
    )(core, table, sink, q, q_other, g, g_other, q.T, q_other.T, g.T, g_other.T, kv)


def shards(queries, key_states, value_states, sink_logit, out_grad, block_table):
    devices = lax.axis_size("seq")
    chips = devices // 2
    me = lax.axis_index("seq")
    chip, core = me // 2, me % 2
    half = HEADS // 2
    half_kv = KV_HEADS // 2
    width = half_kv * HEAD_DIM
    swap = lambda x: lax.ppermute(x, "seq", [(i, i ^ 1) for i in range(devices)])
    groups = [list(range(0, devices, 2)), list(range(1, devices, 2))]
    cut = lambda x, which, size: lax.dynamic_slice_in_dim(x, which * size, size, axis=x.ndim - 1)
    order = lambda mine, theirs: jnp.concatenate(
        [jnp.where(core == 0, mine, theirs), jnp.where(core == 0, theirs, mine)], -1
    )

    kv = jnp.stack([key_states[0], value_states[0]], 0)
    kv_chip = jnp.concatenate([cut(kv, core, width), swap(cut(kv, 1 - core, width))], 1)[None]
    kv_all = lax.all_gather(kv_chip, "seq", axis=0, tiled=True, axis_index_groups=groups)
    q_local, g_local = queries[0], out_grad[0]
    q_other = swap(cut(q_local, 1 - core, half * HEAD_DIM))
    g_other = swap(cut(g_local, 1 - core, half * HEAD_DIM))

    blocks = block_table.shape[1]
    info = jnp.concatenate(
        [
            block_table.astype(jnp.float32).reshape(blocks, KB),
            jnp.broadcast_to(sink_logit.reshape(1, 1), (blocks, 1)),
        ],
        1,
    ).reshape(chips, 1, 2 * (KB + 1))
    info = jnp.broadcast_to(info, (chips, 2, 2 * (KB + 1))).reshape(devices, 2 * (KB + 1))
    info = lax.all_to_all(info, "seq", split_axis=0, concat_axis=0, tiled=True)
    info = lax.dynamic_slice_in_dim(info, core * half, half, axis=0).reshape(half, 2, KB + 1)
    table = info[:, :, :KB].astype(jnp.int32)
    table = jnp.where(core == 0, table, table[:, ::-1]) ^ core
    sink = jnp.broadcast_to(info[:, 0, KB:], (half, BLOCK))
    core_at = core.reshape(1).astype(jnp.int32)
    local = (q_local, q_other, g_local, g_other)
    dq_own, dq_other, dkv, dsink = attention(
        0, jnp.bfloat16, core_at, table.reshape(-1), sink, *local, kv_all
    )
    dkv_chip = lax.psum_scatter(
        dkv, "seq", scatter_dimension=0, tiled=True, axis_index_groups=groups
    )[0]
    sides = (dkv_chip[:, :BLOCK], swap(dkv_chip[:, BLOCK:]))
    key_grad = order(*[x[0] for x in sides])[None]
    value_grad = order(*[x[1] for x in sides])[None]

    query_grad = order(dq_own.T, swap(dq_other).T)[None]

    total = jnp.sum(dsink, 1).reshape(1, half)
    for step in (1, 2, 4, 8):
        total += lax.ppermute(total, "dp", [(i, i ^ step) for i in range(16)])
    for step in (2, 4, 8, 16):
        total += lax.ppermute(total, "seq", [(i, i ^ step) for i in range(devices)])
    sinks = order(total, swap(total)).reshape(HEADS)
    sink_grad = lax.dynamic_slice_in_dim(sinks, me, 1)
    return (query_grad, key_grad, value_grad, sink_grad)


def solution(mesh):
    in_specs = (
        P("dp", "seq", None),
        P("dp", "seq", None),
        P("dp", "seq", None),
        P("seq"),
        P("dp", "seq", None),
        P("seq", None, None),
    )
    out_specs = (P("dp", "seq", None), P("dp", "seq", None), P("dp", "seq", None), P("seq"))
    return jax.shard_map(shards, mesh=mesh, in_specs=in_specs, out_specs=out_specs, check_vma=False)
```

time: 288 us -> 271 us (0.941)
  Pallas kernels: 38.7 us -> 27.1 us
  waiting for transfers between devices: 144 us -> 140 us
    pallas_call x1, Pallas kernels: 38.7 us -> 27.1 us  [attention(): pl.pallas_call(functools.partial(kernel, base), grid_spec=pltpu.PrefetchS...]
    all_to_all x1, waiting for transfers between devices: 5.65 us -> 2.59 us  [shards(): info = lax.all_to_all(info, 'seq', split_axis=0, concat_axis=0, tiled=True)]
    unnamed x21 -> x23, local copies, waits for them, and re-layouts: 6.36 us -> 5.79 us
  transfers between devices with their start and end apart: 17 -> 17, of which waited for: 13 -> 12; matrix products, arithmetic and copies ran while one was open for 2% -> 4% of each run, Pallas kernels for 0% -> 0%
where the time goes in v1:
time: 271 us; the launch traced here: 270 us
  waiting for transfers between devices  140 us (52%)
  starting transfers between devices  70.5 us (26%)
  Pallas kernels  27.1 us (10%)
  local copies, waits for them, and re-layouts  15 us (6%)
  between operations  15 us (6%)
  other arithmetic  2.78 us (1%)
    all_gather x1, waiting for transfers between devices, shards(): lax.all_gather(kv_chip, 'seq', axis=0, tiled=True, axis_index_groups=groups)  78.5 us
    reduce_scatter x1, waiting for transfers between devices, shards(): lax.psum_scatter(dkv, 'seq', scatter_dimension=0, tiled=True, axis_index_...  38.5 us
    ppermute x6, starting transfers between devices, shards(): lax.ppermute(x, 'seq', [(i, i ^ 1) for i in range(devices)])  27.2 us
    pallas_call x1, Pallas kernels, attention(): pl.pallas_call(functools.partial(kernel, base), grid_spec=pltpu.PrefetchS...  27.1 us
    ppermute x4, starting transfers between devices, shards(): total += lax.ppermute(total, 'seq', [(i, i ^ step) for i in range(devices)])  17.8 us
    ppermute x4, starting transfers between devices, shards(): total += lax.ppermute(total, 'dp', [(i, i ^ step) for i in range(16)])  15.1 us
    ppermute x4, waiting for transfers between devices, shards(): total += lax.ppermute(total, 'seq', [(i, i ^ step) for i in range(devices)])  14.3 us
    all_to_all x1, starting transfers between devices, shards(): info = lax.all_to_all(info, 'seq', split_axis=0, concat_axis=0, tiled=True)  10.2 us
  transfers between devices with their start and end apart: 17, of which 12 were waited for; matrix products, arithmetic and copies ran while one was open for 4% of the time, Pallas kernels for 0%

profile of v1, /device:TPU:1, one launch (start us, length us, event | category | flops | bytes accessed | tf_op | source)
XLA Modules:
  0.0 270.5 jit_solution(12475931764199628577)
XLA Ops:
  9.4 8.8 %collective-permute-start.2 = (bf16[2,128,512]{2,1,0:T(8,128)(2,1)S(1)}, bf16[2,128,512]{2,1,0:T(8,128)(2,1)S(1)}, u32[]{:S(2)}, u32[]{:S(2)}) collective-permute-start(bf16[2,128,512]{2,1,0:T(8,128)(2,1)S(1)} %get-tuple-element.35), channel_id=1, source_target_pairs={{0,1},{1,0},{2,3},{3,2},{4,5},{5,4},{6,7},{7,6},{8,9},{9,8},{10,11... | collective-permute-start | bytes 786440 | tf_op jit(solution)/shard_map/ppermute | solution.py:172
  21.7 10.2 %all-to-all-start = ((f32[32,1,18]{2,1,0:T(1,128)}), f32[32,1,18]{2,1,0:T(1,128)S(1)}, u32[]{:S(2)}, u32[]{:S(2)}) async-start(f32[32,1,18]{2,1,0:T(1,128)} %bitcast.4), calls=%async_computation | async-start | bytes 32768 | tf_op jit(solution)/shard_map/all_to_all | solution.py:195
  33.1 2.1 collective-permute-start
  36.3 2.2 collective-permute-start.1
  41.1 2.6 all-to-all-done
  46.9 78.5 %all-gather.3.cloned.1.call-done = bf16[32,256,512]{2,1,0:T(8,128)(2,1)} async-done(((bf16[2,256,512]{2,1,0:T(8,128)(2,1)}), bf16[32,256,512]{2,1,0:T(8,128)(2,1)}) %all-gather.3.cloned.1.call-update) | async-done | bytes 8388624 | tf_op jit(solution)/shard_map/all_gather | solution.py:181
  126.0 27.1 %shard_map.93 = (bf16[2048,128]{1,0:T(8,128)(2,1)}, bf16[2048,128]{1,0:T(8,128)(2,1)}, bf16[16,2,256,512]{3,2,1,0:T(8,128)(2,1)}, f32[16,128]{1,0:T(8,128)}) custom-call(s32[1]{0:T(128)} %bitcast.core_ref, s32[256]{0:T(256)} %reshape.51.table_ref, f32[16,128]{1,0:T(8,128)} %broadcast_in_dim.35.sink_ref, bf16[128,4096]{1,0:T(8,128)(2,1)} %bitcast.43, ...), custom_call_target="tpu_custom_call" | custom-call | flops 10737418240 | bytes 16777216 | tf_op jit(solution)/shard_map/pallas_call | solution.py:132
  153.9 3.1 %collective-permute-start.5 = (f32[1,16]{1,0:T(1,128)S(1)}, f32[1,16]{1,0:T(1,128)S(1)}, u32[]{:S(2)}, u32[]{:S(2)}) collective-permute-start(f32[1,16]{1,0:T(1,128)S(1)} %bitcast.53), channel_id=1, source_target_pairs={{0,32},{32,0},{64,96},{96,64},{128,160},{160,128},{192,224},{224,1... | collective-permute-start | bytes 200 | tf_op jit(solution)/shard_map/ppermute | solution.py:216
  157.0 2.9 %collective-permute-start.3 = (bf16[2048,128]{1,0:T(8,128)(2,1)S(1)}, bf16[2048,128]{1,0:T(8,128)(2,1)S(1)}, u32[]{:S(2)}, u32[]{:S(2)}) collective-permute-start(bf16[2048,128]{1,0:T(8,128)(2,1)S(1)} %copy-done.8), channel_id=1, source_target_pairs={{0,1},{1,0},{2,3},{3,2},{4,5},{5,4},{6,7},{7,6},{8,9},{9,8},{10,11... | collective-permute-start | bytes 1572872 | tf_op jit(solution)/shard_map/ppermute | solution.py:172
  159.9 4.3 %collective-permute-start.6 = (f32[1,16]{1,0:T(1,128)S(1)}, f32[1,16]{1,0:T(1,128)S(1)}, u32[]{:S(2)}, u32[]{:S(2)}) collective-permute-start(f32[1,16]{1,0:T(1,128)S(1)} %bitcast_add_fusion), channel_id=1, source_target_pairs={{0,64},{32,96},{64,0},{96,32},{128,192},{160,224},{192,128},{224,1... | collective-permute-start | bytes 200 | tf_op jit(solution)/shard_map/ppermute | solution.py:216
  165.7 3.1 %collective-permute-start.7 = (f32[1,16]{1,0:T(1,128)S(1)}, f32[1,16]{1,0:T(1,128)S(1)}, u32[]{:S(2)}, u32[]{:S(2)}) collective-permute-start(f32[1,16]{1,0:T(1,128)S(1)} %add.54), channel_id=1, source_target_pairs={{0,128},{32,160},{64,192},{96,224},{128,0},{160,32},{192,64},{224,... | collective-permute-start | bytes 200 | tf_op jit(solution)/shard_map/ppermute | solution.py:216
  168.8 1.6 collective-permute-done.7
  170.4 4.6 %collective-permute-start.8 = (f32[1,16]{1,0:T(1,128)S(1)}, f32[1,16]{1,0:T(1,128)S(1)}, u32[]{:S(2)}, u32[]{:S(2)}) collective-permute-start(f32[1,16]{1,0:T(1,128)S(1)} %add.55), channel_id=1, source_target_pairs={{0,256},{32,288},{64,320},{96,352},{128,384},{160,416},{192,448},{... | collective-permute-start | bytes 200 | tf_op jit(solution)/shard_map/ppermute | solution.py:216
  176.3 1.9 collective-permute-start.9
  178.2 2.9 %collective-permute-done.9 = f32[1,16]{1,0:T(1,128)S(1)} collective-permute-done((f32[1,16]{1,0:T(1,128)S(1)}, f32[1,16]{1,0:T(1,128)S(1)}, u32[]{:S(2)}, u32[]{:S(2)}) %collective-permute-start.9) | collective-permute-done | bytes 96 | tf_op jit(solution)/shard_map/ppermute | solution.py:218
  181.1 2.5 collective-permute-start.10
  183.6 3.2 %collective-permute-done.10 = f32[1,16]{1,0:T(1,128)S(1)} collective-permute-done((f32[1,16]{1,0:T(1,128)S(1)}, f32[1,16]{1,0:T(1,128)S(1)}, u32[]{:S(2)}, u32[]{:S(2)}) %collective-permute-start.10) | collective-permute-done | bytes 96 | tf_op jit(solution)/shard_map/ppermute | solution.py:218
  186.9 4.9 %collective-permute-start.11 = (f32[1,16]{1,0:T(1,128)S(1)}, f32[1,16]{1,0:T(1,128)S(1)}, u32[]{:S(2)}, u32[]{:S(2)}) collective-permute-start(f32[1,16]{1,0:T(1,128)S(1)} %add.58), channel_id=1, source_target_pairs={{0,8},{1,9},{2,10},{3,11},{4,12},{5,13},{6,14},{7,15},{8,0},{9,1},... | collective-permute-start | bytes 200 | tf_op jit(solution)/shard_map/ppermute | solution.py:218
  191.8 3.4 %collective-permute-done.11 = f32[1,16]{1,0:T(1,128)S(1)} collective-permute-done((f32[1,16]{1,0:T(1,128)S(1)}, f32[1,16]{1,0:T(1,128)S(1)}, u32[]{:S(2)}, u32[]{:S(2)}) %collective-permute-start.11) | collective-permute-done | bytes 96 | tf_op jit(solution)/shard_map/ppermute | solution.py:218
  195.2 8.5 %collective-permute-start.12 = (f32[1,16]{1,0:T(1,128)S(1)}, f32[1,16]{1,0:T(1,128)S(1)}, u32[]{:S(2)}, u32[]{:S(2)}) collective-permute-start(f32[1,16]{1,0:T(1,128)S(1)} %add.59), channel_id=1, source_target_pairs={{0,16},{1,17},{2,18},{3,19},{4,20},{5,21},{6,22},{7,23},{8,24},{9,... | collective-permute-start | bytes 200 | tf_op jit(solution)/shard_map/ppermute | solution.py:218
  203.8 4.7 %collective-permute-done.12 = f32[1,16]{1,0:T(1,128)S(1)} collective-permute-done((f32[1,16]{1,0:T(1,128)S(1)}, f32[1,16]{1,0:T(1,128)S(1)}, u32[]{:S(2)}, u32[]{:S(2)}) %collective-permute-start.12) | collective-permute-done | bytes 96 | tf_op jit(solution)/shard_map/ppermute | solution.py:218
  208.4 8.8 %collective-permute-start.13 = (f32[1,16]{1,0:T(1,128)S(1)}, f32[1,16]{1,0:T(1,128)S(1)}, u32[]{:S(2)}, u32[]{:S(2)}) collective-permute-start(f32[1,16]{1,0:T(1,128)S(1)} %add.60), channel_id=1, source_target_pairs={{0,1},{1,0},{2,3},{3,2},{4,5},{5,4},{6,7},{7,6},{8,9},{9,8},{10,11... | collective-permute-start | bytes 200 | tf_op jit(solution)/shard_map/ppermute | solution.py:172
  218.7 38.5 %reduce-scatter.2.cloned.1.call-done = bf16[1,2,256,512]{3,2,1,0:T(8,128)(2,1)} async-done(((bf16[16,2,256,512]{3,2,1,0:T(8,128)(2,1)}), bf16[1,2,256,512]{3,2,1,0:T(8,128)(2,1)}) %reduce-scatter.2.cloned.1.call-update) | async-done | bytes 524304 | tf_op jit(solution)/shard_map/reduce_scatter | solution.py:205
  258.2 2.5 collective-permute-start.4
  (74 shorter events, 22.5 us)
Async XLA Ops:
  7.2 13.7 %copy-start.7 = (s32[1,32,8]{1,2,0:T(8,128)S(1)}, s32[1,32,8]{1,2,0:T(8,128)}, u32[]{:S(2)}) copy-start(s32[1,32,8]{1,2,0:T(8,128)} %param.11) | copy-start | bytes 3076
  7.2 24.8 %copy-start.1 = (bf16[1,128,4096]{2,1,0:T(8,128)(2,1)S(1)}, bf16[1,128,4096]{2,1,0:T(8,128)(2,1)}, u32[]{:S(2)}) copy-start(bf16[1,128,4096]{2,1,0:T(8,128)(2,1)} %param.10) | copy-start | bytes 3145732
  7.2 24.8 %copy-start = (bf16[1,128,4096]{2,1,0:T(8,128)(2,1)S(1)}, bf16[1,128,4096]{2,1,0:T(8,128)(2,1)}, u32[]{:S(2)}) copy-start(bf16[1,128,4096]{2,1,0:T(8,128)(2,1)} %param.6) | copy-start | bytes 3145732
  7.2 118.1 %all-gather.3.cloned.1.call-start = ((), (), s32[]{:S(2)}) async-start(), calls=%async_computation.3 | async-start | bytes 8912896 | tf_op jit(solution)/shard_map/all_gather | solution.py:181
  9.4 9.9 %collective-permute-start.2 = (bf16[2,128,512]{2,1,0:T(8,128)(2,1)S(1)}, bf16[2,128,512]{2,1,0:T(8,128)(2,1)S(1)}, u32[]{:S(2)}, u32[]{:S(2)}) collective-permute-start(bf16[2,128,512]{2,1,0:T(8,128)(2,1)S(1)} %get-tuple-element.35), channel_id=1, source_target_pairs={{0,1},{1,0},{2,3},{3,2},{4,5},{5,4},{6,7},{7,6},{8,9},{9,8},{10,11... | collective-permute-start | bytes 786440 | tf_op jit(solution)/shard_map/ppermute | solution.py:172
  21.7 22.0 %all-to-all-start = ((f32[32,1,18]{2,1,0:T(1,128)}), f32[32,1,18]{2,1,0:T(1,128)S(1)}, u32[]{:S(2)}, u32[]{:S(2)}) async-start(f32[32,1,18]{2,1,0:T(1,128)} %bitcast.4), calls=%async_computation | async-start | bytes 32768 | tf_op jit(solution)/shard_map/all_to_all | solution.py:195
  32.0 225.3 %reduce-scatter.2.cloned.1.call-start = ((), (), s32[]{:S(2)}) async-start(), calls=%async_computation.2 | async-start | bytes 8912896 | tf_op jit(solution)/shard_map/reduce_scatter | solution.py:205
  33.1 11.7 %collective-permute-start = (bf16[128,2048]{0,1:T(8,128)(2,1)}, bf16[128,2048]{0,1:T(8,128)(2,1)S(1)}, u32[]{:S(2)}, u32[]{:S(2)}) collective-permute-start(bf16[128,2048]{0,1:T(8,128)(2,1)} %bitcast.49), channel_id=1, source_target_pairs={{0,1},{1,0},{2,3},{3,2},{4,5},{5,4},{6,7},{7,6},{8,9},{9,8},{10,11... | collective-permute-start | bytes 1572872 | tf_op jit(solution)/shard_map/ppermute | solution.py:172
  36.3 9.6 %collective-permute-start.1 = (bf16[128,2048]{0,1:T(8,128)(2,1)}, bf16[128,2048]{0,1:T(8,128)(2,1)S(1)}, u32[]{:S(2)}, u32[]{:S(2)}) collective-permute-start(bf16[128,2048]{0,1:T(8,128)(2,1)} %bitcast.50), channel_id=1, source_target_pairs={{0,1},{1,0},{2,3},{3,2},{4,5},{5,4},{6,7},{7,6},{8,9},{9,8},{10,11... | collective-permute-start | bytes 1572872 | tf_op jit(solution)/shard_map/ppermute | solution.py:172
  44.8 81.2 %copy-start.3 = (bf16[128,2048]{0,1:T(8,128)(2,1)}, bf16[128,2048]{0,1:T(8,128)(2,1)S(1)}, u32[]{:S(2)}) copy-start(bf16[128,2048]{0,1:T(8,128)(2,1)S(1)} %collective-permute-done) | copy-start | bytes 1572868
  45.9 80.1 %copy-start.4 = (bf16[128,2048]{0,1:T(8,128)(2,1)}, bf16[128,2048]{0,1:T(8,128)(2,1)S(1)}, u32[]{:S(2)}) copy-start(bf16[128,2048]{0,1:T(8,128)(2,1)S(1)} %collective-permute-done.1) | copy-start | bytes 1572868
  153.1 3.9 %copy-start.8 = (bf16[2048,128]{1,0:T(8,128)(2,1)S(1)}, bf16[2048,128]{1,0:T(8,128)(2,1)}, u32[]{:S(2)}) copy-start(bf16[2048,128]{1,0:T(8,128)(2,1)} %get-tuple-element.9) | copy-start | bytes 1572868
  153.1 65.5 %copy-start.2 = (bf16[2048,128]{1,0:T(8,128)(2,1)S(1)}, bf16[2048,128]{1,0:T(8,128)(2,1)}, u32[]{:S(2)}) copy-start(bf16[2048,128]{1,0:T(8,128)(2,1)} %get-tuple-element.8) | copy-start | bytes 1572868
  153.9 6.0 %collective-permute-start.5 = (f32[1,16]{1,0:T(1,128)S(1)}, f32[1,16]{1,0:T(1,128)S(1)}, u32[]{:S(2)}, u32[]{:S(2)}) collective-permute-start(f32[1,16]{1,0:T(1,128)S(1)} %bitcast.53), channel_id=1, source_target_pairs={{0,32},{32,0},{64,96},{96,64},{128,160},{160,128},{192,224},{224,1... | collective-permute-start | bytes 200 | tf_op jit(solution)/shard_map/ppermute | solution.py:216
  157.0 61.6 %collective-permute-start.3 = (bf16[2048,128]{1,0:T(8,128)(2,1)S(1)}, bf16[2048,128]{1,0:T(8,128)(2,1)S(1)}, u32[]{:S(2)}, u32[]{:S(2)}) collective-permute-start(bf16[2048,128]{1,0:T(8,128)(2,1)S(1)} %copy-done.8), channel_id=1, source_target_pairs={{0,1},{1,0},{2,3},{3,2},{4,5},{5,4},{6,7},{7,6},{8,9},{9,8},{10,11... | collective-permute-start | bytes 1572872 | tf_op jit(solution)/shard_map/ppermute | solution.py:172
  159.9 5.8 %collective-permute-start.6 = (f32[1,16]{1,0:T(1,128)S(1)}, f32[1,16]{1,0:T(1,128)S(1)}, u32[]{:S(2)}, u32[]{:S(2)}) collective-permute-start(f32[1,16]{1,0:T(1,128)S(1)} %bitcast_add_fusion), channel_id=1, source_target_pairs={{0,64},{32,96},{64,0},{96,32},{128,192},{160,224},{192,128},{224,1... | collective-permute-start | bytes 200 | tf_op jit(solution)/shard_map/ppermute | solution.py:216
  165.7 4.7 %collective-permute-start.7 = (f32[1,16]{1,0:T(1,128)S(1)}, f32[1,16]{1,0:T(1,128)S(1)}, u32[]{:S(2)}, u32[]{:S(2)}) collective-permute-start(f32[1,16]{1,0:T(1,128)S(1)} %add.54), channel_id=1, source_target_pairs={{0,128},{32,160},{64,192},{96,224},{128,0},{160,32},{192,64},{224,... | collective-permute-start | bytes 200 | tf_op jit(solution)/shard_map/ppermute | solution.py:216
  170.4 5.9 %collective-permute-start.8 = (f32[1,16]{1,0:T(1,128)S(1)}, f32[1,16]{1,0:T(1,128)S(1)}, u32[]{:S(2)}, u32[]{:S(2)}) collective-permute-start(f32[1,16]{1,0:T(1,128)S(1)} %add.55), channel_id=1, source_target_pairs={{0,256},{32,288},{64,320},{96,352},{128,384},{160,416},{192,448},{... | collective-permute-start | bytes 200 | tf_op jit(solution)/shard_map/ppermute | solution.py:216
  176.3 4.8 %collective-permute-start.9 = (f32[1,16]{1,0:T(1,128)S(1)}, f32[1,16]{1,0:T(1,128)S(1)}, u32[]{:S(2)}, u32[]{:S(2)}) collective-permute-start(f32[1,16]{1,0:T(1,128)S(1)} %add.56), channel_id=1, source_target_pairs={{0,2},{1,3},{2,0},{3,1},{4,6},{5,7},{6,4},{7,5},{8,10},{9,11},{10,... | collective-permute-start | bytes 200 | tf_op jit(solution)/shard_map/ppermute | solution.py:218
  181.1 5.7 %collective-permute-start.10 = (f32[1,16]{1,0:T(1,128)S(1)}, f32[1,16]{1,0:T(1,128)S(1)}, u32[]{:S(2)}, u32[]{:S(2)}) collective-permute-start(f32[1,16]{1,0:T(1,128)S(1)} %add.57), channel_id=1, source_target_pairs={{0,4},{1,5},{2,6},{3,7},{4,0},{5,1},{6,2},{7,3},{8,12},{9,13},{10,... | collective-permute-start | bytes 200 | tf_op jit(solution)/shard_map/ppermute | solution.py:218
  186.9 8.4 %collective-permute-start.11 = (f32[1,16]{1,0:T(1,128)S(1)}, f32[1,16]{1,0:T(1,128)S(1)}, u32[]{:S(2)}, u32[]{:S(2)}) collective-permute-start(f32[1,16]{1,0:T(1,128)S(1)} %add.58), channel_id=1, source_target_pairs={{0,8},{1,9},{2,10},{3,11},{4,12},{5,13},{6,14},{7,15},{8,0},{9,1},... | collective-permute-start | bytes 200 | tf_op jit(solution)/shard_map/ppermute | solution.py:218
  195.2 13.2 %collective-permute-start.12 = (f32[1,16]{1,0:T(1,128)S(1)}, f32[1,16]{1,0:T(1,128)S(1)}, u32[]{:S(2)}, u32[]{:S(2)}) collective-permute-start(f32[1,16]{1,0:T(1,128)S(1)} %add.59), channel_id=1, source_target_pairs={{0,16},{1,17},{2,18},{3,19},{4,20},{5,21},{6,22},{7,23},{8,24},{9,... | collective-permute-start | bytes 200 | tf_op jit(solution)/shard_map/ppermute | solution.py:218
  208.4 9.6 %collective-permute-start.13 = (f32[1,16]{1,0:T(1,128)S(1)}, f32[1,16]{1,0:T(1,128)S(1)}, u32[]{:S(2)}, u32[]{:S(2)}) collective-permute-start(f32[1,16]{1,0:T(1,128)S(1)} %add.60), channel_id=1, source_target_pairs={{0,1},{1,0},{2,3},{3,2},{4,5},{5,4},{6,7},{7,6},{8,9},{9,8},{10,11... | collective-permute-start | bytes 200 | tf_op jit(solution)/shard_map/ppermute | solution.py:172
  258.2 3.9 %collective-permute-start.4 = (bf16[2,128,512]{2,1,0:T(8,128)(2,1)S(1)}, bf16[2,128,512]{2,1,0:T(8,128)(2,1)S(1)}, u32[]{:S(2)}, u32[]{:S(2)}) collective-permute-start(bf16[2,128,512]{2,1,0:T(8,128)(2,1)S(1)} %slice.34), channel_id=1, source_target_pairs={{0,1},{1,0},{2,3},{3,2},{4,5},{5,4},{6,7},{7,6},{8,9},{9,8},{10,11... | collective-permute-start | bytes 786440 | tf_op jit(solution)/shard_map/ppermute | solution.py:172
  (2 other events, 2.1 us)
Sparse Core Ops, SparseCore 0:
  20.4 104.9 all-gather.2
  153.3 103.9 reduce-scatter.1

commit v2 on v1

--- a/solution.py
+++ b/solution.py
@@ -19,19 +19,16 @@
 
 
 def kernel(
-    base, core_ref, table_ref, sink_ref, q0_ref, q1_ref, g0_ref, g1_ref,
-    qt0_ref, qt1_ref, gt0_ref, gt1_ref, kv_ref,
+    core_ref, table_ref, sink_ref, q0_ref, q1_ref, g0_ref, g1_ref,
+    qt0_ref, qt1_ref, gt0_ref, gt1_ref, k_ref, v_ref,
     dq0_ref, dq1_ref, dkv_ref, dsink_ref, acc_ref, w_ref, wt_ref, kt_ref,
 ):
-    chips = kv_ref.shape[0]
-    local = pl.program_id(0)
-    kv_head = base + local
+    kv_head = pl.program_id(0)
     acc_ref[...] = jnp.zeros_like(acc_ref)
     w_ref[...] = jnp.zeros_like(w_ref)
     wt_ref[...] = jnp.zeros_like(wt_ref)
-    for c in range(chips):
-        for s in range(2):
-            kt_ref[c, s] = kv_ref[c, 0, s * BLOCK : (s + 1) * BLOCK, :].T
+    for c in range(k_ref.shape[0]):
+        kt_ref[c] = k_ref[c].T
     refs = (
         (q0_ref, g0_ref, qt0_ref, gt0_ref, dq0_ref),
         (q1_ref, g1_ref, qt1_ref, gt1_ref, dq1_ref),
@@ -51,12 +48,12 @@
             places, both = [], []
             for b in range(KB):
                 block = table_ref[((kv_head * GROUP + j) * 2 + s) * KB + b]
-                chip, slot = block >> 1, block & 1
-                rows = pl.ds(pl.multiple_of(slot * BLOCK, BLOCK), BLOCK)
-                places.append((chip, slot, rows))
-                kv = jnp.concatenate([kv_ref[chip, 0, rows, :], kv_ref[chip, 1, rows, :]], 1)
+                place = block ^ core_ref[0]
+                rows = pl.ds(pl.multiple_of((place & 1) * BLOCK, BLOCK), BLOCK)
+                places.append((block, place >> 1, rows))
+                kv = jnp.concatenate([k_ref[block], v_ref[block]], 1)
                 both.append(jnp.dot(kv, wt, preferred_element_type=jnp.float32))
-            sink = sink_ref[pl.ds(kv_head * GROUP + j, 1), :] * LOG2E
+            sink = sink_ref[kv_head * GROUP + j] * LOG2E
             return at, places, both, sink
 
         def middle(both, sink):
@@ -84,14 +81,13 @@
 
         def last(i, s, at, places, terms):
             w = w_ref[i]
-            for (chip, _, rows), pair in zip(places, terms):
+            for (_, chip, rows), pair in zip(places, terms):
                 acc_ref[chip, rows, :] += jnp.dot(
                     jnp.concatenate(pair, 1), w, preferred_element_type=jnp.float32
                 )
             dq = jnp.zeros((HEAD_DIM, BLOCK), jnp.float32)
             for b in range(0, KB, 2):
-                (chip0, slot0, _), (chip1, slot1, _) = places[b], places[b + 1]
-                kt = jnp.concatenate([kt_ref[chip0, slot0], kt_ref[chip1, slot1]], 1)
+                kt = jnp.concatenate([kt_ref[places[b][0]], kt_ref[places[b + 1][0]]], 1)
                 ds = jnp.concatenate([terms[b][0], terms[b + 1][0]], 0)
                 dq += jnp.dot(kt, ds, preferred_element_type=jnp.float32)
             refs[s][4][at, :] = (dq * SCALE).astype(jnp.bfloat16)
@@ -107,7 +103,7 @@
             last(k % 4, k % 2, at, places, terms)
             held = later
         for u in range(UNROLL):
-            row = pl.ds(local * GROUP + step * UNROLL + u, 1)
+            row = pl.ds(kv_head * GROUP + step * UNROLL + u, 1)
             dsink_ref[row, :] = -(sinks[2 * u] + sinks[2 * u + 1])
         return 0
 
@@ -116,49 +112,56 @@
     dkv_ref[:, 1] = acc_ref[:, :, HEAD_DIM:].astype(dkv_ref.dtype)
 
 
-def attention(base, kind, core, table, sink, q, q_other, g, g_other, kv):
-    chips, heads_here = kv.shape[0], kv.shape[3] // HEAD_DIM
+def attention(core, table, sink, q, q_other, g, g_other, kv):
+    blocks = kv.shape[0]
+    chips = blocks // 2
     kv_heads = KV_HEADS // 2
     wide = GROUP * HEAD_DIM
     half = HEADS // 2
-    fixed = lambda i, core, table: (0, 0)
-    big = pl.BlockSpec((chips, 2, 2 * BLOCK, HEAD_DIM), lambda i, core, table: (0, 0, 0, i))
-    own = pl.BlockSpec((BLOCK, wide), lambda i, core, table: (0, core[0] * kv_heads + base + i))
-    other = pl.BlockSpec((BLOCK, wide), lambda i, core, table: (0, base + i))
-    own_t = pl.BlockSpec((wide, BLOCK), lambda i, core, table: (core[0] * kv_heads + base + i, 0))
-    other_t = pl.BlockSpec((wide, BLOCK), lambda i, core, table: (base + i, 0))
-    out_t = pl.BlockSpec((wide, BLOCK), lambda i, core, table: (i, 0))
-    pairs = heads_here * GROUP * 2
+    fixed = lambda i, core, table, sink: (0, 0)
+    keys = pl.BlockSpec(
+        (blocks, BLOCK, HEAD_DIM), lambda i, core, table, sink: (0, 0, core[0] * kv_heads + i)
+    )
+    values = pl.BlockSpec(
+        (blocks, BLOCK, HEAD_DIM),
+        lambda i, core, table, sink: (0, 0, KV_HEADS + core[0] * kv_heads + i),
+    )
+    big = pl.BlockSpec((chips, 2, 2 * BLOCK, HEAD_DIM), lambda i, core, table, sink: (0, 0, 0, i))
+    own = pl.BlockSpec((BLOCK, wide), lambda i, core, table, sink: (0, core[0] * kv_heads + i))
+    other = pl.BlockSpec((BLOCK, wide), lambda i, core, table, sink: (0, i))
+    own_t = pl.BlockSpec((wide, BLOCK), lambda i, core, table, sink: (core[0] * kv_heads + i, 0))
+    other_t = pl.BlockSpec((wide, BLOCK), lambda i, core, table, sink: (i, 0))
+    out_t = pl.BlockSpec((wide, BLOCK), lambda i, core, table, sink: (i, 0))
+    pairs = kv_heads * GROUP * 2
     return pl.pallas_call(
-        functools.partial(kernel, base),
+        kernel,
         grid_spec=pltpu.PrefetchScalarGridSpec(
-            num_scalar_prefetch=2,
-            grid=(heads_here,),
+            num_scalar_prefetch=3,
+            grid=(kv_heads,),
             in_specs=[
-                pl.BlockSpec((half, BLOCK), fixed),
-                own, other, own, other, own_t, other_t, own_t, other_t, big,
+                own, other, own, other, own_t, other_t, own_t, other_t, keys, values,
             ],
-            out_specs=[out_t, out_t, big, pl.BlockSpec((heads_here * GROUP, BLOCK), fixed)],
+            out_specs=[out_t, out_t, big, pl.BlockSpec((kv_heads * GROUP, BLOCK), fixed)],
             scratch_shapes=[
                 pltpu.VMEM((chips, 2 * BLOCK, 2 * HEAD_DIM), jnp.float32),
                 pltpu.VMEM((4, 2 * BLOCK, 2 * HEAD_DIM), jnp.bfloat16),
                 pltpu.VMEM((4, 2 * HEAD_DIM, 2 * BLOCK), jnp.bfloat16),
-                pltpu.VMEM((chips, 2, HEAD_DIM, BLOCK), jnp.bfloat16),
+                pltpu.VMEM((blocks, HEAD_DIM, BLOCK), jnp.bfloat16),
             ],
         ),
         out_shape=[
-            jax.ShapeDtypeStruct((heads_here * wide, BLOCK), jnp.bfloat16),
-            jax.ShapeDtypeStruct((heads_here * wide, BLOCK), jnp.bfloat16),
-            jax.ShapeDtypeStruct((chips, 2, 2 * BLOCK, heads_here * HEAD_DIM), kind),
-            jax.ShapeDtypeStruct((heads_here * GROUP, BLOCK), jnp.float32),
+            jax.ShapeDtypeStruct((kv_heads * wide, BLOCK), jnp.bfloat16),
+            jax.ShapeDtypeStruct((kv_heads * wide, BLOCK), jnp.bfloat16),
+            jax.ShapeDtypeStruct((chips, 2, 2 * BLOCK, kv_heads * HEAD_DIM), jnp.bfloat16),
+            jax.ShapeDtypeStruct((kv_heads * GROUP, BLOCK), jnp.float32),
         ],
         compiler_params=pltpu.CompilerParams(vmem_limit_bytes=58 * 2**20),
         cost_estimate=pl.CostEstimate(
             flops=2 * 10 * pairs * BLOCK * KB * BLOCK * HEAD_DIM,
-            bytes_accessed=2 * 2 * chips * 2 * 2 * BLOCK * heads_here * HEAD_DIM,
+            bytes_accessed=2 * 2 * chips * 2 * 2 * BLOCK * kv_heads * HEAD_DIM,
             transcendentals=pairs * BLOCK * KB * BLOCK,
         ),
-    )(core, table, sink, q, q_other, g, g_other, q.T, q_other.T, g.T, g_other.T, kv)
+    )(core, table, sink, q, q_other, g, g_other, q.T, q_other.T, g.T, g_other.T, kv, kv)
 
 
 def shards(queries, key_states, value_states, sink_logit, out_grad, block_table):
@@ -167,8 +170,6 @@
     me = lax.axis_index("seq")
     chip, core = me // 2, me % 2
     half = HEADS // 2
-    half_kv = KV_HEADS // 2
-    width = half_kv * HEAD_DIM
     swap = lambda x: lax.ppermute(x, "seq", [(i, i ^ 1) for i in range(devices)])
     groups = [list(range(0, devices, 2)), list(range(1, devices, 2))]
     cut = lambda x, which, size: lax.dynamic_slice_in_dim(x, which * size, size, axis=x.ndim - 1)
@@ -176,9 +177,8 @@
         [jnp.where(core == 0, mine, theirs), jnp.where(core == 0, theirs, mine)], -1
     )
 
-    kv = jnp.stack([key_states[0], value_states[0]], 0)
-    kv_chip = jnp.concatenate([cut(kv, core, width), swap(cut(kv, 1 - core, width))], 1)[None]
-    kv_all = lax.all_gather(kv_chip, "seq", axis=0, tiled=True, axis_index_groups=groups)
+    kv_all = lax.all_gather(jnp.concatenate([key_states, value_states], 2), "seq", axis=0, tiled=True)
+
     q_local, g_local = queries[0], out_grad[0]
     q_other = swap(cut(q_local, 1 - core, half * HEAD_DIM))
     g_other = swap(cut(g_local, 1 - core, half * HEAD_DIM))
@@ -195,12 +195,12 @@
     info = lax.all_to_all(info, "seq", split_axis=0, concat_axis=0, tiled=True)
     info = lax.dynamic_slice_in_dim(info, core * half, half, axis=0).reshape(half, 2, KB + 1)
     table = info[:, :, :KB].astype(jnp.int32)
-    table = jnp.where(core == 0, table, table[:, ::-1]) ^ core
-    sink = jnp.broadcast_to(info[:, 0, KB:], (half, BLOCK))
+    table = jnp.where(core == 0, table, table[:, ::-1])
+    sink = info[:, 0, KB]
     core_at = core.reshape(1).astype(jnp.int32)
     local = (q_local, q_other, g_local, g_other)
     dq_own, dq_other, dkv, dsink = attention(
-        0, jnp.bfloat16, core_at, table.reshape(-1), sink, *local, kv_all
+        core_at, table.reshape(-1), sink, *local, kv_all
     )
     dkv_chip = lax.psum_scatter(
         dkv, "seq", scatter_dimension=0, tiled=True, axis_index_groups=groups

time: 271 us -> 266 us (0.982)
  starting transfers between devices: 70.5 us -> 67.7 us
    ppermute x6 -> x5, starting transfers between devices: 27.2 us -> 18 us  [shards(): lax.ppermute(x, 'seq', [(i, i ^ 1) for i in range(devices)])]
    all_to_all x1, starting transfers between devices: 10.2 us -> 16.7 us  [shards(): info = lax.all_to_all(info, 'seq', split_axis=0, concat_axis=0, tiled=True)]
    unnamed x23 -> x20, local copies, waits for them, and re-layouts: 5.79 us -> 4.73 us
  transfers between devices with their start and end apart: 17 -> 16, of which waited for: 12 -> 11; matrix products, arithmetic and copies ran while one was open for 4% -> 5% of each run, Pallas kernels for 0% -> 0%
where the time goes in v2:
time: 266 us
  waiting for transfers between devices  139 us (52%)
  starting transfers between devices  67.7 us (25%)
  Pallas kernels  26 us (10%)
  between operations  15 us (6%)
  local copies, waits for them, and re-layouts  13.8 us (5%)
  other arithmetic  4.53 us (2%)
    all_gather x1, waiting for transfers between devices, shards(): lax.all_gather(jnp.concatenate([key_states, value_states], 2), 'seq', axi...  79.3 us
    reduce_scatter x1, waiting for transfers between devices, shards(): lax.psum_scatter(dkv, 'seq', scatter_dimension=0, tiled=True, axis_index_...  38.5 us
    pallas_call x1, Pallas kernels, attention(): pl.pallas_call(kernel, grid_spec=pltpu.PrefetchScalarGridSpec(num_scalar_...  26 us
    ppermute x5, starting transfers between devices, shards(): lax.ppermute(x, 'seq', [(i, i ^ 1) for i in range(devices)])  18 us
    ppermute x4, starting transfers between devices, shards(): total += lax.ppermute(total, 'seq', [(i, i ^ step) for i in range(devices)])  17.7 us
    all_to_all x1, starting transfers between devices, shards(): info = lax.all_to_all(info, 'seq', split_axis=0, concat_axis=0, tiled=True)  16.7 us
    ppermute x4, starting transfers between devices, shards(): total += lax.ppermute(total, 'dp', [(i, i ^ step) for i in range(16)])  15.1 us
    ppermute x4, waiting for transfers between devices, shards(): total += lax.ppermute(total, 'seq', [(i, i ^ step) for i in range(devices)])  14.4 us
  transfers between devices with their start and end apart: 16, of which 11 were waited for; matrix products, arithmetic and copies ran while one was open for 5% of the time, Pallas kernels for 0%

profile of v2, /device:TPU:1, one launch (start us, length us, event | category | flops | bytes accessed | tf_op | source)
XLA Modules:
  0.0 265.8 jit_solution(11094708705799940338)
XLA Ops:
  7.2 2.0 pad_maximum_fusion
  11.3 16.7 %all-to-all-start = ((f32[32,1,18]{2,1,0:T(1,128)}), f32[32,1,18]{2,1,0:T(1,128)S(1)}, u32[]{:S(2)}, u32[]{:S(2)}) async-start(f32[32,1,18]{2,1,0:T(1,128)} %bitcast.4), calls=%async_computation | async-start | bytes 32768 | tf_op jit(solution)/shard_map/all_to_all | solution.py:195
  30.3 2.1 collective-permute-start
  33.4 2.2 collective-permute-start.1
  38.3 1.5 all-to-all-done
  43.5 79.3 %all-gather.2.cloned.1.call-done.k_ref.v_ref = bf16[32,128,2048]{2,1,0:T(8,128)(2,1)} async-done(((bf16[1,128,2048]{2,1,0:T(8,128)(2,1)}), bf16[32,128,2048]{2,1,0:T(8,128)(2,1)}) %all-gather.2.cloned.1.call-update) | async-done | bytes 16777232 | tf_op jit(solution)/shard_map/all_gather | solution.py:180
  122.9 26.0 %shard_map.93 = (bf16[2048,128]{1,0:T(8,128)(2,1)}, bf16[2048,128]{1,0:T(8,128)(2,1)}, bf16[16,2,256,512]{3,2,1,0:T(8,128)(2,1)}, f32[16,128]{1,0:T(8,128)}) custom-call(s32[1]{0:T(128)} %bitcast.core_ref, s32[256]{0:T(256)} %reshape.50.table_ref, f32[16]{0:T(128)} %slice_reduce_fusion.sink_ref, bf16[128,4096]{1,0:T(8,128)(2,1)} %bitcast.42, ...), custom_call_target="tpu_custom_call" | custom-call | flops 10737418240 | bytes 16777216 | tf_op jit(solution)/shard_map/pallas_call | solution.py:136
  149.7 3.1 %collective-permute-start.4 = (f32[1,16]{1,0:T(1,128)S(1)}, f32[1,16]{1,0:T(1,128)S(1)}, u32[]{:S(2)}, u32[]{:S(2)}) collective-permute-start(f32[1,16]{1,0:T(1,128)S(1)} %bitcast.52), channel_id=1, source_target_pairs={{0,32},{32,0},{64,96},{96,64},{128,160},{160,128},{192,224},{224,1... | collective-permute-start | bytes 200 | tf_op jit(solution)/shard_map/ppermute | solution.py:216
  152.8 2.4 collective-permute-start.2
  155.3 4.3 %collective-permute-start.5 = (f32[1,16]{1,0:T(1,128)S(1)}, f32[1,16]{1,0:T(1,128)S(1)}, u32[]{:S(2)}, u32[]{:S(2)}) collective-permute-start(f32[1,16]{1,0:T(1,128)S(1)} %bitcast_add_fusion), channel_id=1, source_target_pairs={{0,64},{32,96},{64,0},{96,32},{128,192},{160,224},{192,128},{224,1... | collective-permute-start | bytes 200 | tf_op jit(solution)/shard_map/ppermute | solution.py:216
  161.1 3.1 %collective-permute-start.6 = (f32[1,16]{1,0:T(1,128)S(1)}, f32[1,16]{1,0:T(1,128)S(1)}, u32[]{:S(2)}, u32[]{:S(2)}) collective-permute-start(f32[1,16]{1,0:T(1,128)S(1)} %add.46), channel_id=1, source_target_pairs={{0,128},{32,160},{64,192},{96,224},{128,0},{160,32},{192,64},{224,... | collective-permute-start | bytes 200 | tf_op jit(solution)/shard_map/ppermute | solution.py:216
  164.2 1.6 collective-permute-done.6
  165.8 4.6 %collective-permute-start.7 = (f32[1,16]{1,0:T(1,128)S(1)}, f32[1,16]{1,0:T(1,128)S(1)}, u32[]{:S(2)}, u32[]{:S(2)}) collective-permute-start(f32[1,16]{1,0:T(1,128)S(1)} %add.47), channel_id=1, source_target_pairs={{0,256},{32,288},{64,320},{96,352},{128,384},{160,416},{192,448},{... | collective-permute-start | bytes 200 | tf_op jit(solution)/shard_map/ppermute | solution.py:216
  171.6 1.9 collective-permute-start.8
  173.5 2.9 %collective-permute-done.8 = f32[1,16]{1,0:T(1,128)S(1)} collective-permute-done((f32[1,16]{1,0:T(1,128)S(1)}, f32[1,16]{1,0:T(1,128)S(1)}, u32[]{:S(2)}, u32[]{:S(2)}) %collective-permute-start.8) | collective-permute-done | bytes 96 | tf_op jit(solution)/shard_map/ppermute | solution.py:218
  176.5 2.5 collective-permute-start.9
  178.9 3.3 %collective-permute-done.9 = f32[1,16]{1,0:T(1,128)S(1)} collective-permute-done((f32[1,16]{1,0:T(1,128)S(1)}, f32[1,16]{1,0:T(1,128)S(1)}, u32[]{:S(2)}, u32[]{:S(2)}) %collective-permute-start.9) | collective-permute-done | bytes 96 | tf_op jit(solution)/shard_map/ppermute | solution.py:218
  182.2 4.9 %collective-permute-start.10 = (f32[1,16]{1,0:T(1,128)S(1)}, f32[1,16]{1,0:T(1,128)S(1)}, u32[]{:S(2)}, u32[]{:S(2)}) collective-permute-start(f32[1,16]{1,0:T(1,128)S(1)} %add.50), channel_id=1, source_target_pairs={{0,8},{1,9},{2,10},{3,11},{4,12},{5,13},{6,14},{7,15},{8,0},{9,1},... | collective-permute-start | bytes 200 | tf_op jit(solution)/shard_map/ppermute | solution.py:218
  187.1 3.5 %collective-permute-done.10 = f32[1,16]{1,0:T(1,128)S(1)} collective-permute-done((f32[1,16]{1,0:T(1,128)S(1)}, f32[1,16]{1,0:T(1,128)S(1)}, u32[]{:S(2)}, u32[]{:S(2)}) %collective-permute-start.10) | collective-permute-done | bytes 96 | tf_op jit(solution)/shard_map/ppermute | solution.py:218
  190.6 8.5 %collective-permute-start.11 = (f32[1,16]{1,0:T(1,128)S(1)}, f32[1,16]{1,0:T(1,128)S(1)}, u32[]{:S(2)}, u32[]{:S(2)}) collective-permute-start(f32[1,16]{1,0:T(1,128)S(1)} %add.51), channel_id=1, source_target_pairs={{0,16},{1,17},{2,18},{3,19},{4,20},{5,21},{6,22},{7,23},{8,24},{9,... | collective-permute-start | bytes 200 | tf_op jit(solution)/shard_map/ppermute | solution.py:218
  199.1 4.7 %collective-permute-done.11 = f32[1,16]{1,0:T(1,128)S(1)} collective-permute-done((f32[1,16]{1,0:T(1,128)S(1)}, f32[1,16]{1,0:T(1,128)S(1)}, u32[]{:S(2)}, u32[]{:S(2)}) %collective-permute-start.11) | collective-permute-done | bytes 96 | tf_op jit(solution)/shard_map/ppermute | solution.py:218
  203.8 8.7 %collective-permute-start.12 = (f32[1,16]{1,0:T(1,128)S(1)}, f32[1,16]{1,0:T(1,128)S(1)}, u32[]{:S(2)}, u32[]{:S(2)}) collective-permute-start(f32[1,16]{1,0:T(1,128)S(1)} %add.52), channel_id=1, source_target_pairs={{0,1},{1,0},{2,3},{3,2},{4,5},{5,4},{6,7},{7,6},{8,9},{9,8},{10,11... | collective-permute-start | bytes 200 | tf_op jit(solution)/shard_map/ppermute | solution.py:173
  214.1 38.5 %reduce-scatter.2.cloned.1.call-done = bf16[1,2,256,512]{3,2,1,0:T(8,128)(2,1)} async-done(((bf16[16,2,256,512]{3,2,1,0:T(8,128)(2,1)}), bf16[1,2,256,512]{3,2,1,0:T(8,128)(2,1)}) %reduce-scatter.2.cloned.1.call-update) | async-done | bytes 524304 | tf_op jit(solution)/shard_map/reduce_scatter | solution.py:205
  253.5 2.5 collective-permute-start.3
  (66 shorter events, 20.0 us)
Async XLA Ops:
  7.2 21.0 %copy-start = (bf16[1,128,4096]{2,1,0:T(8,128)(2,1)S(1)}, bf16[1,128,4096]{2,1,0:T(8,128)(2,1)}, u32[]{:S(2)}) copy-start(bf16[1,128,4096]{2,1,0:T(8,128)(2,1)} %param.6) | copy-start | bytes 3145732
  7.2 115.7 %all-gather.2.cloned.1.call-start = ((), (), s32[]{:S(2)}) async-start(), calls=%async_computation.2 | async-start | bytes 17301504 | tf_op jit(solution)/shard_map/all_gather | solution.py:180
  11.3 28.5 %all-to-all-start = ((f32[32,1,18]{2,1,0:T(1,128)}), f32[32,1,18]{2,1,0:T(1,128)S(1)}, u32[]{:S(2)}, u32[]{:S(2)}) async-start(f32[32,1,18]{2,1,0:T(1,128)} %bitcast.4), calls=%async_computation | async-start | bytes 32768 | tf_op jit(solution)/shard_map/all_to_all | solution.py:195
  28.1 224.5 %reduce-scatter.2.cloned.1.call-start = ((), (), s32[]{:S(2)}) async-start(), calls=%async_computation.3 | async-start | bytes 8912896 | tf_op jit(solution)/shard_map/reduce_scatter | solution.py:205
  29.3 7.7 %copy-start.1 = (bf16[1,128,4096]{2,1,0:T(8,128)(2,1)S(1)}, bf16[1,128,4096]{2,1,0:T(8,128)(2,1)}, u32[]{:S(2)}) copy-start(bf16[1,128,4096]{2,1,0:T(8,128)(2,1)} %param.10) | copy-start | bytes 3145732
  30.3 11.2 %collective-permute-start = (bf16[128,2048]{0,1:T(8,128)(2,1)}, bf16[128,2048]{0,1:T(8,128)(2,1)S(1)}, u32[]{:S(2)}, u32[]{:S(2)}) collective-permute-start(bf16[128,2048]{0,1:T(8,128)(2,1)} %bitcast.48), channel_id=1, source_target_pairs={{0,1},{1,0},{2,3},{3,2},{4,5},{5,4},{6,7},{7,6},{8,9},{9,8},{10,11... | collective-permute-start | bytes 1572872 | tf_op jit(solution)/shard_map/ppermute | solution.py:173
  33.4 9.0 %collective-permute-start.1 = (bf16[128,2048]{0,1:T(8,128)(2,1)}, bf16[128,2048]{0,1:T(8,128)(2,1)S(1)}, u32[]{:S(2)}, u32[]{:S(2)}) collective-permute-start(bf16[128,2048]{0,1:T(8,128)(2,1)} %bitcast.49), channel_id=1, source_target_pairs={{0,1},{1,0},{2,3},{3,2},{4,5},{5,4},{6,7},{7,6},{8,9},{9,8},{10,11... | collective-permute-start | bytes 1572872 | tf_op jit(solution)/shard_map/ppermute | solution.py:173
  41.5 81.4 %copy-start.2 = (bf16[128,2048]{0,1:T(8,128)(2,1)}, bf16[128,2048]{0,1:T(8,128)(2,1)S(1)}, u32[]{:S(2)}) copy-start(bf16[128,2048]{0,1:T(8,128)(2,1)S(1)} %collective-permute-done) | copy-start | bytes 1572868
  42.5 80.4 %copy-start.3 = (bf16[128,2048]{0,1:T(8,128)(2,1)}, bf16[128,2048]{0,1:T(8,128)(2,1)S(1)}, u32[]{:S(2)}) copy-start(bf16[128,2048]{0,1:T(8,128)(2,1)S(1)} %collective-permute-done.1) | copy-start | bytes 1572868
  148.9 0.7 copy-start.6
  148.9 3.9 %copy-start.7 = (bf16[2048,128]{1,0:T(8,128)(2,1)S(1)}, bf16[2048,128]{1,0:T(8,128)(2,1)}, u32[]{:S(2)}) copy-start(bf16[2048,128]{1,0:T(8,128)(2,1)} %get-tuple-element.9) | copy-start | bytes 1572868
  148.9 65.1 %copy-start.4 = (bf16[2048,128]{1,0:T(8,128)(2,1)S(1)}, bf16[2048,128]{1,0:T(8,128)(2,1)}, u32[]{:S(2)}) copy-start(bf16[2048,128]{1,0:T(8,128)(2,1)} %get-tuple-element.8) | copy-start | bytes 1572868
  149.7 5.6 %collective-permute-start.4 = (f32[1,16]{1,0:T(1,128)S(1)}, f32[1,16]{1,0:T(1,128)S(1)}, u32[]{:S(2)}, u32[]{:S(2)}) collective-permute-start(f32[1,16]{1,0:T(1,128)S(1)} %bitcast.52), channel_id=1, source_target_pairs={{0,32},{32,0},{64,96},{96,64},{128,160},{160,128},{192,224},{224,1... | collective-permute-start | bytes 200 | tf_op jit(solution)/shard_map/ppermute | solution.py:216
  152.8 61.2 %collective-permute-start.2 = (bf16[2048,128]{1,0:T(8,128)(2,1)S(1)}, bf16[2048,128]{1,0:T(8,128)(2,1)S(1)}, u32[]{:S(2)}, u32[]{:S(2)}) collective-permute-start(bf16[2048,128]{1,0:T(8,128)(2,1)S(1)} %copy-done.7), channel_id=1, source_target_pairs={{0,1},{1,0},{2,3},{3,2},{4,5},{5,4},{6,7},{7,6},{8,9},{9,8},{10,11... | collective-permute-start | bytes 1572872 | tf_op jit(solution)/shard_map/ppermute | solution.py:173
  155.3 5.8 %collective-permute-start.5 = (f32[1,16]{1,0:T(1,128)S(1)}, f32[1,16]{1,0:T(1,128)S(1)}, u32[]{:S(2)}, u32[]{:S(2)}) collective-permute-start(f32[1,16]{1,0:T(1,128)S(1)} %bitcast_add_fusion), channel_id=1, source_target_pairs={{0,64},{32,96},{64,0},{96,32},{128,192},{160,224},{192,128},{224,1... | collective-permute-start | bytes 200 | tf_op jit(solution)/shard_map/ppermute | solution.py:216
  161.1 4.7 %collective-permute-start.6 = (f32[1,16]{1,0:T(1,128)S(1)}, f32[1,16]{1,0:T(1,128)S(1)}, u32[]{:S(2)}, u32[]{:S(2)}) collective-permute-start(f32[1,16]{1,0:T(1,128)S(1)} %add.46), channel_id=1, source_target_pairs={{0,128},{32,160},{64,192},{96,224},{128,0},{160,32},{192,64},{224,... | collective-permute-start | bytes 200 | tf_op jit(solution)/shard_map/ppermute | solution.py:216
  165.8 5.9 %collective-permute-start.7 = (f32[1,16]{1,0:T(1,128)S(1)}, f32[1,16]{1,0:T(1,128)S(1)}, u32[]{:S(2)}, u32[]{:S(2)}) collective-permute-start(f32[1,16]{1,0:T(1,128)S(1)} %add.47), channel_id=1, source_target_pairs={{0,256},{32,288},{64,320},{96,352},{128,384},{160,416},{192,448},{... | collective-permute-start | bytes 200 | tf_op jit(solution)/shard_map/ppermute | solution.py:216
  171.6 4.8 %collective-permute-start.8 = (f32[1,16]{1,0:T(1,128)S(1)}, f32[1,16]{1,0:T(1,128)S(1)}, u32[]{:S(2)}, u32[]{:S(2)}) collective-permute-start(f32[1,16]{1,0:T(1,128)S(1)} %add.48), channel_id=1, source_target_pairs={{0,2},{1,3},{2,0},{3,1},{4,6},{5,7},{6,4},{7,5},{8,10},{9,11},{10,... | collective-permute-start | bytes 200 | tf_op jit(solution)/shard_map/ppermute | solution.py:218
  176.5 5.7 %collective-permute-start.9 = (f32[1,16]{1,0:T(1,128)S(1)}, f32[1,16]{1,0:T(1,128)S(1)}, u32[]{:S(2)}, u32[]{:S(2)}) collective-permute-start(f32[1,16]{1,0:T(1,128)S(1)} %add.49), channel_id=1, source_target_pairs={{0,4},{1,5},{2,6},{3,7},{4,0},{5,1},{6,2},{7,3},{8,12},{9,13},{10,... | collective-permute-start | bytes 200 | tf_op jit(solution)/shard_map/ppermute | solution.py:218
  182.2 8.4 %collective-permute-start.10 = (f32[1,16]{1,0:T(1,128)S(1)}, f32[1,16]{1,0:T(1,128)S(1)}, u32[]{:S(2)}, u32[]{:S(2)}) collective-permute-start(f32[1,16]{1,0:T(1,128)S(1)} %add.50), channel_id=1, source_target_pairs={{0,8},{1,9},{2,10},{3,11},{4,12},{5,13},{6,14},{7,15},{8,0},{9,1},... | collective-permute-start | bytes 200 | tf_op jit(solution)/shard_map/ppermute | solution.py:218
  190.6 13.2 %collective-permute-start.11 = (f32[1,16]{1,0:T(1,128)S(1)}, f32[1,16]{1,0:T(1,128)S(1)}, u32[]{:S(2)}, u32[]{:S(2)}) collective-permute-start(f32[1,16]{1,0:T(1,128)S(1)} %add.51), channel_id=1, source_target_pairs={{0,16},{1,17},{2,18},{3,19},{4,20},{5,21},{6,22},{7,23},{8,24},{9,... | collective-permute-start | bytes 200 | tf_op jit(solution)/shard_map/ppermute | solution.py:218
  203.8 9.5 %collective-permute-start.12 = (f32[1,16]{1,0:T(1,128)S(1)}, f32[1,16]{1,0:T(1,128)S(1)}, u32[]{:S(2)}, u32[]{:S(2)}) collective-permute-start(f32[1,16]{1,0:T(1,128)S(1)} %add.52), channel_id=1, source_target_pairs={{0,1},{1,0},{2,3},{3,2},{4,5},{5,4},{6,7},{7,6},{8,9},{9,8},{10,11... | collective-permute-start | bytes 200 | tf_op jit(solution)/shard_map/ppermute | solution.py:173
  253.5 3.9 %collective-permute-start.3 = (bf16[2,128,512]{2,1,0:T(8,128)(2,1)S(1)}, bf16[2,128,512]{2,1,0:T(8,128)(2,1)S(1)}, u32[]{:S(2)}, u32[]{:S(2)}) collective-permute-start(bf16[2,128,512]{2,1,0:T(8,128)(2,1)S(1)} %slice.34), channel_id=1, source_target_pairs={{0,1},{1,0},{2,3},{3,2},{4,5},{5,4},{6,7},{7,6},{8,9},{9,8},{10,11... | collective-permute-start | bytes 786440 | tf_op jit(solution)/shard_map/ppermute | solution.py:173
  256.0 1.4 copy-start.5
Sparse Core Ops, SparseCore 0:
  10.1 112.6 all-gather.1
  149.0 103.4 reduce-scatter.1

commit v3 on v2

--- a/solution.py
+++ b/solution.py
@@ -94,14 +94,15 @@
 
         count = 2 * UNROLL
         held = first(0, 0)
+        next1 = first(0, 1)
         sinks = []
         for k in range(count):
-            later = first((k + 1) // 2, (k + 1) % 2) if k + 1 < count else None
+            later = first((k + 2) // 2, (k + 2) % 2) if k + 2 < count else None
             at, places, both, sink = held
             terms, sink_term = middle(both, sink)
             sinks.append(sink_term)
             last(k % 4, k % 2, at, places, terms)
-            held = later
+            held, next1 = next1, later
         for u in range(UNROLL):
             row = pl.ds(kv_head * GROUP + step * UNROLL + u, 1)
             dsink_ref[row, :] = -(sinks[2 * u] + sinks[2 * u + 1])

time: 266 us -> 267 us (level)
  no operation moved by 1% of the time
where the time goes in v3:
time: 267 us; the launch traced here: 266 us
  waiting for transfers between devices  139 us (52%)
  starting transfers between devices  67.7 us (25%)
  Pallas kernels  26.1 us (10%)
  between operations  15 us (6%)
  local copies, waits for them, and re-layouts  13.8 us (5%)
  other arithmetic  4.53 us (2%)
    all_gather x1, waiting for transfers between devices, shards(): lax.all_gather(jnp.concatenate([key_states, value_states], 2), 'seq', axi...  79.3 us
    reduce_scatter x1, waiting for transfers between devices, shards(): lax.psum_scatter(dkv, 'seq', scatter_dimension=0, tiled=True, axis_index_...  38.5 us
    pallas_call x1, Pallas kernels, attention(): pl.pallas_call(kernel, grid_spec=pltpu.PrefetchScalarGridSpec(num_scalar_...  26.1 us
    ppermute x5, starting transfers between devices, shards(): lax.ppermute(x, 'seq', [(i, i ^ 1) for i in range(devices)])  18 us
    ppermute x4, starting transfers between devices, shards(): total += lax.ppermute(total, 'seq', [(i, i ^ step) for i in range(devices)])  17.7 us
    all_to_all x1, starting transfers between devices, shards(): info = lax.all_to_all(info, 'seq', split_axis=0, concat_axis=0, tiled=True)  16.7 us
    ppermute x4, starting transfers between devices, shards(): total += lax.ppermute(total, 'dp', [(i, i ^ step) for i in range(16)])  15.1 us
    ppermute x4, waiting for transfers between devices, shards(): total += lax.ppermute(total, 'seq', [(i, i ^ step) for i in range(devices)])  14.4 us
  transfers between devices with their start and end apart: 16, of which 11 were waited for; matrix products, arithmetic and copies ran while one was open for 5% of the time, Pallas kernels for 0%

profile of v3, /device:TPU:1, one launch (start us, length us, event | category | flops | bytes accessed | tf_op | source)
XLA Modules:
  0.0 265.9 jit_solution(12247761045876119444)
XLA Ops:
  7.2 2.0 pad_maximum_fusion
  11.3 16.7 %all-to-all-start = ((f32[32,1,18]{2,1,0:T(1,128)}), f32[32,1,18]{2,1,0:T(1,128)S(1)}, u32[]{:S(2)}, u32[]{:S(2)}) async-start(f32[32,1,18]{2,1,0:T(1,128)} %bitcast.4), calls=%async_computation | async-start | bytes 32768 | tf_op jit(solution)/shard_map/all_to_all | solution.py:196
  30.3 2.1 collective-permute-start
  33.4 2.2 collective-permute-start.1
  38.3 1.5 all-to-all-done
  43.5 79.3 %all-gather.2.cloned.1.call-done.k_ref.v_ref = bf16[32,128,2048]{2,1,0:T(8,128)(2,1)} async-done(((bf16[1,128,2048]{2,1,0:T(8,128)(2,1)}), bf16[32,128,2048]{2,1,0:T(8,128)(2,1)}) %all-gather.2.cloned.1.call-update) | async-done | bytes 16777232 | tf_op jit(solution)/shard_map/all_gather | solution.py:181
  122.9 26.1 %shard_map.93 = (bf16[2048,128]{1,0:T(8,128)(2,1)}, bf16[2048,128]{1,0:T(8,128)(2,1)}, bf16[16,2,256,512]{3,2,1,0:T(8,128)(2,1)}, f32[16,128]{1,0:T(8,128)}) custom-call(s32[1]{0:T(128)} %bitcast.core_ref, s32[256]{0:T(256)} %reshape.50.table_ref, f32[16]{0:T(128)} %slice_reduce_fusion.sink_ref, bf16[128,4096]{1,0:T(8,128)(2,1)} %bitcast.42, ...), custom_call_target="tpu_custom_call" | custom-call | flops 10737418240 | bytes 16777216 | tf_op jit(solution)/shard_map/pallas_call | solution.py:137
  149.8 3.1 %collective-permute-start.4 = (f32[1,16]{1,0:T(1,128)S(1)}, f32[1,16]{1,0:T(1,128)S(1)}, u32[]{:S(2)}, u32[]{:S(2)}) collective-permute-start(f32[1,16]{1,0:T(1,128)S(1)} %bitcast.52), channel_id=1, source_target_pairs={{0,32},{32,0},{64,96},{96,64},{128,160},{160,128},{192,224},{224,1... | collective-permute-start | bytes 200 | tf_op jit(solution)/shard_map/ppermute | solution.py:217
  152.9 2.4 collective-permute-start.2
  155.4 4.3 %collective-permute-start.5 = (f32[1,16]{1,0:T(1,128)S(1)}, f32[1,16]{1,0:T(1,128)S(1)}, u32[]{:S(2)}, u32[]{:S(2)}) collective-permute-start(f32[1,16]{1,0:T(1,128)S(1)} %bitcast_add_fusion), channel_id=1, source_target_pairs={{0,64},{32,96},{64,0},{96,32},{128,192},{160,224},{192,128},{224,1... | collective-permute-start | bytes 200 | tf_op jit(solution)/shard_map/ppermute | solution.py:217
  161.2 3.1 %collective-permute-start.6 = (f32[1,16]{1,0:T(1,128)S(1)}, f32[1,16]{1,0:T(1,128)S(1)}, u32[]{:S(2)}, u32[]{:S(2)}) collective-permute-start(f32[1,16]{1,0:T(1,128)S(1)} %add.46), channel_id=1, source_target_pairs={{0,128},{32,160},{64,192},{96,224},{128,0},{160,32},{192,64},{224,... | collective-permute-start | bytes 200 | tf_op jit(solution)/shard_map/ppermute | solution.py:217
  164.3 1.6 collective-permute-done.6
  165.9 4.6 %collective-permute-start.7 = (f32[1,16]{1,0:T(1,128)S(1)}, f32[1,16]{1,0:T(1,128)S(1)}, u32[]{:S(2)}, u32[]{:S(2)}) collective-permute-start(f32[1,16]{1,0:T(1,128)S(1)} %add.47), channel_id=1, source_target_pairs={{0,256},{32,288},{64,320},{96,352},{128,384},{160,416},{192,448},{... | collective-permute-start | bytes 200 | tf_op jit(solution)/shard_map/ppermute | solution.py:217
  171.7 1.9 collective-permute-start.8
  173.6 2.9 %collective-permute-done.8 = f32[1,16]{1,0:T(1,128)S(1)} collective-permute-done((f32[1,16]{1,0:T(1,128)S(1)}, f32[1,16]{1,0:T(1,128)S(1)}, u32[]{:S(2)}, u32[]{:S(2)}) %collective-permute-start.8) | collective-permute-done | bytes 96 | tf_op jit(solution)/shard_map/ppermute | solution.py:219
  176.6 2.5 collective-permute-start.9
  179.0 3.3 %collective-permute-done.9 = f32[1,16]{1,0:T(1,128)S(1)} collective-permute-done((f32[1,16]{1,0:T(1,128)S(1)}, f32[1,16]{1,0:T(1,128)S(1)}, u32[]{:S(2)}, u32[]{:S(2)}) %collective-permute-start.9) | collective-permute-done | bytes 96 | tf_op jit(solution)/shard_map/ppermute | solution.py:219
  182.3 4.9 %collective-permute-start.10 = (f32[1,16]{1,0:T(1,128)S(1)}, f32[1,16]{1,0:T(1,128)S(1)}, u32[]{:S(2)}, u32[]{:S(2)}) collective-permute-start(f32[1,16]{1,0:T(1,128)S(1)} %add.50), channel_id=1, source_target_pairs={{0,8},{1,9},{2,10},{3,11},{4,12},{5,13},{6,14},{7,15},{8,0},{9,1},... | collective-permute-start | bytes 200 | tf_op jit(solution)/shard_map/ppermute | solution.py:219
  187.2 3.5 %collective-permute-done.10 = f32[1,16]{1,0:T(1,128)S(1)} collective-permute-done((f32[1,16]{1,0:T(1,128)S(1)}, f32[1,16]{1,0:T(1,128)S(1)}, u32[]{:S(2)}, u32[]{:S(2)}) %collective-permute-start.10) | collective-permute-done | bytes 96 | tf_op jit(solution)/shard_map/ppermute | solution.py:219
  190.7 8.5 %collective-permute-start.11 = (f32[1,16]{1,0:T(1,128)S(1)}, f32[1,16]{1,0:T(1,128)S(1)}, u32[]{:S(2)}, u32[]{:S(2)}) collective-permute-start(f32[1,16]{1,0:T(1,128)S(1)} %add.51), channel_id=1, source_target_pairs={{0,16},{1,17},{2,18},{3,19},{4,20},{5,21},{6,22},{7,23},{8,24},{9,... | collective-permute-start | bytes 200 | tf_op jit(solution)/shard_map/ppermute | solution.py:219
  199.2 4.7 %collective-permute-done.11 = f32[1,16]{1,0:T(1,128)S(1)} collective-permute-done((f32[1,16]{1,0:T(1,128)S(1)}, f32[1,16]{1,0:T(1,128)S(1)}, u32[]{:S(2)}, u32[]{:S(2)}) %collective-permute-start.11) | collective-permute-done | bytes 96 | tf_op jit(solution)/shard_map/ppermute | solution.py:219
  203.9 8.7 %collective-permute-start.12 = (f32[1,16]{1,0:T(1,128)S(1)}, f32[1,16]{1,0:T(1,128)S(1)}, u32[]{:S(2)}, u32[]{:S(2)}) collective-permute-start(f32[1,16]{1,0:T(1,128)S(1)} %add.52), channel_id=1, source_target_pairs={{0,1},{1,0},{2,3},{3,2},{4,5},{5,4},{6,7},{7,6},{8,9},{9,8},{10,11... | collective-permute-start | bytes 200 | tf_op jit(solution)/shard_map/ppermute | solution.py:174
  214.2 38.5 %reduce-scatter.2.cloned.1.call-done = bf16[1,2,256,512]{3,2,1,0:T(8,128)(2,1)} async-done(((bf16[16,2,256,512]{3,2,1,0:T(8,128)(2,1)}), bf16[1,2,256,512]{3,2,1,0:T(8,128)(2,1)}) %reduce-scatter.2.cloned.1.call-update) | async-done | bytes 524304 | tf_op jit(solution)/shard_map/reduce_scatter | solution.py:206
  253.6 2.5 collective-permute-start.3
  (66 shorter events, 20.0 us)
Async XLA Ops:
  7.2 21.0 %copy-start = (bf16[1,128,4096]{2,1,0:T(8,128)(2,1)S(1)}, bf16[1,128,4096]{2,1,0:T(8,128)(2,1)}, u32[]{:S(2)}) copy-start(bf16[1,128,4096]{2,1,0:T(8,128)(2,1)} %param.6) | copy-start | bytes 3145732
  7.2 115.7 %all-gather.2.cloned.1.call-start = ((), (), s32[]{:S(2)}) async-start(), calls=%async_computation.2 | async-start | bytes 17301504 | tf_op jit(solution)/shard_map/all_gather | solution.py:181
  11.3 28.5 %all-to-all-start = ((f32[32,1,18]{2,1,0:T(1,128)}), f32[32,1,18]{2,1,0:T(1,128)S(1)}, u32[]{:S(2)}, u32[]{:S(2)}) async-start(f32[32,1,18]{2,1,0:T(1,128)} %bitcast.4), calls=%async_computation | async-start | bytes 32768 | tf_op jit(solution)/shard_map/all_to_all | solution.py:196
  28.1 224.6 %reduce-scatter.2.cloned.1.call-start = ((), (), s32[]{:S(2)}) async-start(), calls=%async_computation.3 | async-start | bytes 8912896 | tf_op jit(solution)/shard_map/reduce_scatter | solution.py:206
  29.3 7.7 %copy-start.1 = (bf16[1,128,4096]{2,1,0:T(8,128)(2,1)S(1)}, bf16[1,128,4096]{2,1,0:T(8,128)(2,1)}, u32[]{:S(2)}) copy-start(bf16[1,128,4096]{2,1,0:T(8,128)(2,1)} %param.10) | copy-start | bytes 3145732
  30.3 11.2 %collective-permute-start = (bf16[128,2048]{0,1:T(8,128)(2,1)}, bf16[128,2048]{0,1:T(8,128)(2,1)S(1)}, u32[]{:S(2)}, u32[]{:S(2)}) collective-permute-start(bf16[128,2048]{0,1:T(8,128)(2,1)} %bitcast.48), channel_id=1, source_target_pairs={{0,1},{1,0},{2,3},{3,2},{4,5},{5,4},{6,7},{7,6},{8,9},{9,8},{10,11... | collective-permute-start | bytes 1572872 | tf_op jit(solution)/shard_map/ppermute | solution.py:174
  33.4 9.0 %collective-permute-start.1 = (bf16[128,2048]{0,1:T(8,128)(2,1)}, bf16[128,2048]{0,1:T(8,128)(2,1)S(1)}, u32[]{:S(2)}, u32[]{:S(2)}) collective-permute-start(bf16[128,2048]{0,1:T(8,128)(2,1)} %bitcast.49), channel_id=1, source_target_pairs={{0,1},{1,0},{2,3},{3,2},{4,5},{5,4},{6,7},{7,6},{8,9},{9,8},{10,11... | collective-permute-start | bytes 1572872 | tf_op jit(solution)/shard_map/ppermute | solution.py:174
  41.5 81.4 %copy-start.2 = (bf16[128,2048]{0,1:T(8,128)(2,1)}, bf16[128,2048]{0,1:T(8,128)(2,1)S(1)}, u32[]{:S(2)}) copy-start(bf16[128,2048]{0,1:T(8,128)(2,1)S(1)} %collective-permute-done) | copy-start | bytes 1572868
  42.5 80.4 %copy-start.3 = (bf16[128,2048]{0,1:T(8,128)(2,1)}, bf16[128,2048]{0,1:T(8,128)(2,1)S(1)}, u32[]{:S(2)}) copy-start(bf16[128,2048]{0,1:T(8,128)(2,1)S(1)} %collective-permute-done.1) | copy-start | bytes 1572868
  149.0 0.7 copy-start.6
  149.0 3.9 %copy-start.7 = (bf16[2048,128]{1,0:T(8,128)(2,1)S(1)}, bf16[2048,128]{1,0:T(8,128)(2,1)}, u32[]{:S(2)}) copy-start(bf16[2048,128]{1,0:T(8,128)(2,1)} %get-tuple-element.9) | copy-start | bytes 1572868
  149.0 65.1 %copy-start.4 = (bf16[2048,128]{1,0:T(8,128)(2,1)S(1)}, bf16[2048,128]{1,0:T(8,128)(2,1)}, u32[]{:S(2)}) copy-start(bf16[2048,128]{1,0:T(8,128)(2,1)} %get-tuple-element.8) | copy-start | bytes 1572868
  149.8 5.6 %collective-permute-start.4 = (f32[1,16]{1,0:T(1,128)S(1)}, f32[1,16]{1,0:T(1,128)S(1)}, u32[]{:S(2)}, u32[]{:S(2)}) collective-permute-start(f32[1,16]{1,0:T(1,128)S(1)} %bitcast.52), channel_id=1, source_target_pairs={{0,32},{32,0},{64,96},{96,64},{128,160},{160,128},{192,224},{224,1... | collective-permute-start | bytes 200 | tf_op jit(solution)/shard_map/ppermute | solution.py:217
  152.9 61.2 %collective-permute-start.2 = (bf16[2048,128]{1,0:T(8,128)(2,1)S(1)}, bf16[2048,128]{1,0:T(8,128)(2,1)S(1)}, u32[]{:S(2)}, u32[]{:S(2)}) collective-permute-start(bf16[2048,128]{1,0:T(8,128)(2,1)S(1)} %copy-done.7), channel_id=1, source_target_pairs={{0,1},{1,0},{2,3},{3,2},{4,5},{5,4},{6,7},{7,6},{8,9},{9,8},{10,11... | collective-permute-start | bytes 1572872 | tf_op jit(solution)/shard_map/ppermute | solution.py:174
  155.4 5.8 %collective-permute-start.5 = (f32[1,16]{1,0:T(1,128)S(1)}, f32[1,16]{1,0:T(1,128)S(1)}, u32[]{:S(2)}, u32[]{:S(2)}) collective-permute-start(f32[1,16]{1,0:T(1,128)S(1)} %bitcast_add_fusion), channel_id=1, source_target_pairs={{0,64},{32,96},{64,0},{96,32},{128,192},{160,224},{192,128},{224,1... | collective-permute-start | bytes 200 | tf_op jit(solution)/shard_map/ppermute | solution.py:217
  161.2 4.7 %collective-permute-start.6 = (f32[1,16]{1,0:T(1,128)S(1)}, f32[1,16]{1,0:T(1,128)S(1)}, u32[]{:S(2)}, u32[]{:S(2)}) collective-permute-start(f32[1,16]{1,0:T(1,128)S(1)} %add.46), channel_id=1, source_target_pairs={{0,128},{32,160},{64,192},{96,224},{128,0},{160,32},{192,64},{224,... | collective-permute-start | bytes 200 | tf_op jit(solution)/shard_map/ppermute | solution.py:217
  165.9 5.9 %collective-permute-start.7 = (f32[1,16]{1,0:T(1,128)S(1)}, f32[1,16]{1,0:T(1,128)S(1)}, u32[]{:S(2)}, u32[]{:S(2)}) collective-permute-start(f32[1,16]{1,0:T(1,128)S(1)} %add.47), channel_id=1, source_target_pairs={{0,256},{32,288},{64,320},{96,352},{128,384},{160,416},{192,448},{... | collective-permute-start | bytes 200 | tf_op jit(solution)/shard_map/ppermute | solution.py:217
  171.7 4.8 %collective-permute-start.8 = (f32[1,16]{1,0:T(1,128)S(1)}, f32[1,16]{1,0:T(1,128)S(1)}, u32[]{:S(2)}, u32[]{:S(2)}) collective-permute-start(f32[1,16]{1,0:T(1,128)S(1)} %add.48), channel_id=1, source_target_pairs={{0,2},{1,3},{2,0},{3,1},{4,6},{5,7},{6,4},{7,5},{8,10},{9,11},{10,... | collective-permute-start | bytes 200 | tf_op jit(solution)/shard_map/ppermute | solution.py:219
  176.6 5.7 %collective-permute-start.9 = (f32[1,16]{1,0:T(1,128)S(1)}, f32[1,16]{1,0:T(1,128)S(1)}, u32[]{:S(2)}, u32[]{:S(2)}) collective-permute-start(f32[1,16]{1,0:T(1,128)S(1)} %add.49), channel_id=1, source_target_pairs={{0,4},{1,5},{2,6},{3,7},{4,0},{5,1},{6,2},{7,3},{8,12},{9,13},{10,... | collective-permute-start | bytes 200 | tf_op jit(solution)/shard_map/ppermute | solution.py:219
  182.3 8.4 %collective-permute-start.10 = (f32[1,16]{1,0:T(1,128)S(1)}, f32[1,16]{1,0:T(1,128)S(1)}, u32[]{:S(2)}, u32[]{:S(2)}) collective-permute-start(f32[1,16]{1,0:T(1,128)S(1)} %add.50), channel_id=1, source_target_pairs={{0,8},{1,9},{2,10},{3,11},{4,12},{5,13},{6,14},{7,15},{8,0},{9,1},... | collective-permute-start | bytes 200 | tf_op jit(solution)/shard_map/ppermute | solution.py:219
  190.7 13.2 %collective-permute-start.11 = (f32[1,16]{1,0:T(1,128)S(1)}, f32[1,16]{1,0:T(1,128)S(1)}, u32[]{:S(2)}, u32[]{:S(2)}) collective-permute-start(f32[1,16]{1,0:T(1,128)S(1)} %add.51), channel_id=1, source_target_pairs={{0,16},{1,17},{2,18},{3,19},{4,20},{5,21},{6,22},{7,23},{8,24},{9,... | collective-permute-start | bytes 200 | tf_op jit(solution)/shard_map/ppermute | solution.py:219
  203.9 9.5 %collective-permute-start.12 = (f32[1,16]{1,0:T(1,128)S(1)}, f32[1,16]{1,0:T(1,128)S(1)}, u32[]{:S(2)}, u32[]{:S(2)}) collective-permute-start(f32[1,16]{1,0:T(1,128)S(1)} %add.52), channel_id=1, source_target_pairs={{0,1},{1,0},{2,3},{3,2},{4,5},{5,4},{6,7},{7,6},{8,9},{9,8},{10,11... | collective-permute-start | bytes 200 | tf_op jit(solution)/shard_map/ppermute | solution.py:174
  253.6 3.9 %collective-permute-start.3 = (bf16[2,128,512]{2,1,0:T(8,128)(2,1)S(1)}, bf16[2,128,512]{2,1,0:T(8,128)(2,1)S(1)}, u32[]{:S(2)}, u32[]{:S(2)}) collective-permute-start(bf16[2,128,512]{2,1,0:T(8,128)(2,1)S(1)} %slice.34), channel_id=1, source_target_pairs={{0,1},{1,0},{2,3},{3,2},{4,5},{5,4},{6,7},{7,6},{8,9},{9,8},{10,11... | collective-permute-start | bytes 786440 | tf_op jit(solution)/shard_map/ppermute | solution.py:174
  256.1 1.4 copy-start.5
Sparse Core Ops, SparseCore 0:
  10.1 112.6 all-gather.1
  149.1 103.4 reduce-scatter.1
